TPU v7x, 512 devices: a whole 4x4x16 slice. The times are simulated.
512 devices in a mesh: src: 32 (over y, z_lo), slab: 16 (over z_hi, x, core).
Axes of the slice: x: 4, y: 4, z: 16 (z_hi: 2, z_lo: 8; z = z_hi * 8 + z_lo), core: 2. Of those that a mesh axis runs over, the one named last changes fastest.
Arguments:
- source_field: float32 [32, 16, 25600], P('src', 'slab'), may hold values from -6 to 6
- kappa: float32 [16, 25600], P('slab'), may hold values from 0.5 to 2
- absorb: float32 [16, 25600], P('slab'), may hold values from 0.02 to 0.2
- det_cell: int32 [512], replicated, may hold values from 0 to 409599
- pair_det: int32 [32, 256], P('src'), may hold values from 0 to 511
- pair_count: int32 [32], P('src'), may hold values from 1 to 256, as said below
- measured: float32 [2, 32, 256], P(None, 'src'), may hold values from -6 to 6
Outputs:
- grad_absorb: float32 [16, 25600], P('slab', 'src')
- grad_diffuse: float32 [16, 25600], P('slab', 'src')
Inputs may be any that keep to these rules, and one draw needn't show every extreme that they name: `pair_count`: some source has exactly 256 live pairs in every draw.
All inputs are finite; a program needn't handle non-finite values.
Results may differ from a plain program's by a relative error of at most 0.0003.
Values sent between devices are 32-bit elements; how exact they have to be, the bound alone decides.
A program may use at most 128 MiB of HBM per device.

v0:
```python
import jax
import jax.numpy as jnp
from jax import lax
from jax.sharding import PartitionSpec as P

NY = 160
SWEEPS = 6
NDET = 512


spectrum_low = 0.02
spectrum_high = 25.0
frequency_shift = 0.3


def padded_2(cells, sides, width):
    for axis, dim in sides:
        count = lax.axis_size(axis)
        ends = count - 1
        head = lax.slice_in_dim(cells, 0, width, axis=dim)
        tail = lax.slice_in_dim(cells, cells.shape[dim] - width, cells.shape[dim], axis=dim)
        cells = jnp.concatenate(
            [
                lax.ppermute(tail, axis, [(i, (i + 1) % count) for i in range(ends)]),
                cells,
                lax.ppermute(head, axis, [((i + 1) % count, i) for i in range(ends)]),
            ],
            axis=dim,
        )
    return cells


def chebyshev_terms():
    theta = (spectrum_high + spectrum_low) / 2.0
    delta = (spectrum_high - spectrum_low) / 2.0
    sigma = theta / delta
    rho = 1.0 / sigma
    keeps = []
    pushes = []
    for sweep in range(SWEEPS - 1):
        rho_new = 1.0 / (2.0 * sigma - rho)
        keeps.append(rho_new * rho)
        pushes.append(2.0 * rho_new / delta)
        rho = rho_new
    return (1.0 / theta, keeps, pushes)


def widen(field):
    return padded_2(field, (("slab", 2),), 1)


def body(source_field, kappa, absorb, det_cell, pair_det, pair_count, measured):
    depth, plane = kappa.shape
    count_src = source_field.shape[0]
    flat = jnp.arange(plane)
    row_index = flat // NY
    col_index = flat % NY
    mask_xm = (row_index > 0).astype(jnp.float32)
    mask_xp = (row_index < plane // NY - 1).astype(jnp.float32)
    mask_ym = (col_index > 0).astype(jnp.float32)
    mask_yp = (col_index < NY - 1).astype(jnp.float32)
    shifts = ((NY, mask_xm), (-NY, mask_xp), (1, mask_ym), (-1, mask_yp))
    kappa_pad = padded_2(kappa, (("slab", 0),), 1)
    plane_faces = []
    diagonal = absorb
    for amount, mask in shifts:
        face = (kappa + jnp.roll(kappa, amount, axis=1) * mask) * 0.5
        diagonal = diagonal + face
        plane_faces.append(face * mask)
    face_zm = (kappa + kappa_pad[:-2]) * 0.5
    face_zp = (kappa + kappa_pad[2:]) * 0.5
    diagonal = diagonal + face_zm + face_zp

    def apply_operator(padded):
        field = padded[:, :, 1:-1]
        offdiag = face_zm * padded[:, :, :-2] + face_zp * padded[:, :, 2:]
        for which in range(4):
            offdiag = offdiag + plane_faces[which] * jnp.roll(field, shifts[which][0], axis=3)
        turned = jnp.stack([-field[:, 1], field[:, 0]], axis=1)
        return diagonal * field - offdiag + frequency_shift * turned

    first, keeps, pushes = chebyshev_terms()

    def solve(right):
        residual_field = right
        direction = right * first
        solution = jnp.zeros_like(right)
        for sweep in range(SWEEPS):
            direction_pad = widen(direction)
            solution = solution + direction
            residual_field = residual_field - apply_operator(direction_pad)
            if sweep < SWEEPS - 1:
                direction = keeps[sweep] * direction + pushes[sweep] * residual_field
        return solution

    def solve_all(right):
        return solve(right)

    forward_right = jnp.stack([source_field, jnp.zeros_like(source_field)], axis=1)
    forward_out = solve_all(forward_right)
    offset = lax.axis_index("slab") * (depth * plane)
    local_cell = det_cell - offset
    inside = (local_cell >= 0) & (local_cell < depth * plane)
    safe_cell = jnp.where(inside, local_cell, 0)
    inside_f = inside.astype(jnp.float32)
    local_read = forward_out.reshape(count_src, 2, depth * plane)[:, :, safe_cell] * inside_f
    readings = lax.psum(local_read, "slab")
    index_pairs = jnp.broadcast_to(pair_det[:, None, :], (count_src, 2, pair_det.shape[1]))
    optical_model = jnp.take_along_axis(readings, index_pairs, axis=2)
    active_flag = (jnp.arange(pair_det.shape[1])[None, :] < pair_count[:, None]).astype(jnp.float32)
    measurement_data = jnp.moveaxis(measured, 0, 1)
    residual_field = (optical_model - measurement_data) * active_flag[:, None, :]
    conj = residual_field * jnp.array([1.0, -1.0], jnp.float32)[None, :, None]
    onehot = (pair_det[:, :, None] == jnp.arange(NDET)[None, None, :]).astype(jnp.float32)
    weights = jnp.einsum("scp,spd->scd", conj, onehot, precision=lax.Precision.HIGHEST)
    adjoint_right = (
        jnp.zeros((count_src, 2, depth * plane), jnp.float32)
        .at[:, :, safe_cell]
        .add(weights * inside_f)
    )
    adjoint_out = solve_all(adjoint_right.reshape(count_src, 2, depth, plane))
    both = padded_2(jnp.concatenate([forward_out, adjoint_out], axis=0), (("slab", 2),), 1)
    forward_pad = both[:count_src]
    adjoint_pad = both[count_src:]
    fwd = forward_pad[:, :, 1:-1]
    adj = adjoint_pad[:, :, 1:-1]
    g_abs = -jnp.sum(fwd[:, 0] * adj[:, 0] - fwd[:, 1] * adj[:, 1], axis=0)
    total = (fwd - forward_pad[:, :, :-2]) * (adj - adjoint_pad[:, :, :-2])
    total = total + (fwd - forward_pad[:, :, 2:]) * (adj - adjoint_pad[:, :, 2:])
    for amount, mask in shifts:
        total = total + (fwd - jnp.roll(fwd, amount, axis=3) * mask) * (
            adj - jnp.roll(adj, amount, axis=3) * mask
        )
    g_dif = -0.5 * jnp.sum(total[:, 0] - total[:, 1], axis=0)
    terms = jnp.stack([g_abs, g_dif])
    summed = lax.psum_scatter(terms, "src", scatter_dimension=2, tiled=True)
    return (summed[0], summed[1])


def solution(mesh):
    placed = (
        P("src", "slab", None),
        P("slab", None),
        P("slab", None),
        P(),
        P("src", None),
        P("src"),
        P(None, "src", None),
    )
    return jax.shard_map(
        body,
        mesh=mesh,
        in_specs=placed,
        out_specs=(P("slab", "src"), P("slab", "src")),
        check_vma=False,
    )
```

profile of v0, /device:TPU:1, one launch (start us, length us, event | category | flops | bytes accessed | tf_op | source)
XLA Modules:
  0.0 840.2 jit_solution(12304161318979065087)
XLA Ops:
  7.2 4.5 collective-permute-start
  11.7 5.6 collective-permute-start.1
  18.3 1.9 collective-permute-start.3
  20.3 3.6 collective-permute-start.2
  23.9 1.3 fusion.189
  27.3 1.2 fusion.190
  28.9 1.2 fusion.188
  33.5 4.6 add_add_fusion
  38.9 1.9 fusion.6
  41.1 1.9 collective-permute-start.5
  43.0 3.6 collective-permute-start.4
  48.2 1.2 collective-permute-done.4
  50.7 1.9 collective-permute-start.7
  52.6 4.4 collective-permute-start.6
  58.5 1.2 collective-permute-done.6
  60.9 1.9 collective-permute-start.9
  62.9 4.4 collective-permute-start.8
  68.8 1.2 collective-permute-done.8
  71.2 1.9 collective-permute-start.11
  73.2 4.6 collective-permute-start.10
  79.1 1.2 collective-permute-done.10
  80.3 2.6 fusion.49
  83.6 6.9 copy.265
  90.5 5.8 gather_fusion
  96.4 154.5 %psum.7 = f32[1,2,512]{1,2,0:T(8,128)S(1)} all-reduce(f32[1,2,512]{1,2,0:T(8,128)S(1)} %bitcast_multiply_fusion), channel_id=1, replica_groups=mesh['src'=32,'slab'=16] {'slab'}, use_global_device_ids=true, to_apply=%region_0.1 | all-reduce | flops 1024 | bytes 8192 | tf_op jit(solution)/shard_map/psum | solution.py:107
  250.9 3.9 gather_fusion.1
  255.4 9.4 %scatter_custom_fusion = f32[2,25600]{0,1:T(8,128)} fusion(s32[512]{0:T(512)S(1)} %compare_select_fusion.8, f32[512,2]{1,0:T(8,128)S(1)} %copy.266, f32[]{:T(128)} %constant.28.clone.1), kind=kCustom, calls=%fused_computation.4 | custom fusion | flops 1024 | bytes 204804 | tf_op jit(solution)/shard_map/scatter-add | solution.py:119
  264.8 7.6 copy.267
  272.7 6.8 collective-permute-start.13
  279.6 9.4 %collective-permute-start.12 = (f32[1,2,1,25600]{3,1,2,0:T(2,128)S(1)}, f32[1,2,1,25600]{3,1,2,0:T(2,128)S(1)}, u32[]{:S(2)}, u32[]{:S(2)}) collective-permute-start(f32[1,2,1,25600]{3,1,2,0:T(2,128)S(1)} %bitcast_multiply_fusion.3), channel_id=1, source_target_pairs={{0,1},{1,2},{2,3},{3,4},{4,5},{5,6},{6,7},{7,8},{8,9},{9,10},{10,1... | collective-permute-start | bytes 614408 | tf_op jit(solution)/shard_map/ppermute | solution.py:24
  290.4 1.2 collective-permute-done.12
  292.9 1.9 collective-permute-start.15
  294.8 4.9 collective-permute-start.14
  303.2 1.9 collective-permute-start.17
  305.1 11.2 %collective-permute-start.16 = (f32[1,2,1,25600]{3,1,2,0:T(2,128)S(1)}, f32[1,2,1,25600]{3,1,2,0:T(2,128)S(1)}, u32[]{:S(2)}, u32[]{:S(2)}) collective-permute-start(f32[1,2,1,25600]{3,1,2,0:T(2,128)S(1)} %get-tuple-element.6), channel_id=1, source_target_pairs={{0,1},{1,2},{2,3},{3,4},{4,5},{5,6},{6,7},{7,8},{8,9},{9,10},{10,1... | collective-permute-start | bytes 614408 | tf_op jit(solution)/shard_map/ppermute | solution.py:24
  320.3 1.9 collective-permute-start.19
  322.2 4.4 collective-permute-start.18
  330.6 1.9 collective-permute-start.21
  332.5 11.0 %collective-permute-start.20 = (f32[1,2,1,25600]{3,1,2,0:T(2,128)S(1)}, f32[1,2,1,25600]{3,1,2,0:T(2,128)S(1)}, u32[]{:S(2)}, u32[]{:S(2)}) collective-permute-start(f32[1,2,1,25600]{3,1,2,0:T(2,128)S(1)} %get-tuple-element.2), channel_id=1, source_target_pairs={{0,1},{1,2},{2,3},{3,4},{4,5},{5,6},{6,7},{7,8},{8,9},{9,10},{10,1... | collective-permute-start | bytes 614408 | tf_op jit(solution)/shard_map/ppermute | solution.py:24
  346.2 2.6 fusion.87
  349.8 1.9 collective-permute-start.23
  351.7 4.6 collective-permute-start.22
  356.4 3.4 collective-permute-done.23
  361.0 2.6 fusion.99
  363.9 22.7 %copy.268 = f32[2,1,25600]{1,0,2:T(2,128)} copy(f32[2,1,25600]{2,1,0:T(1,128)S(1)} %pad_maximum_fusion.1) | data formatting | bytes 409600
  386.6 49.0 %bitcast_reduce_fusion = f32[25600,2]{1,0:T(8,128)} fusion(f32[2,1,25600]{1,0,2:T(2,128)} %copy.268), kind=kLoop, calls=%fused_computation.3 | loop fusion | bytes 409600
  435.6 392.9 %reduce-scatter.4.cloned.1.call-done = f32[800,2]{1,0:T(8,128)} async-done(((f32[25600,2]{1,0:T(8,128)}), f32[800,2]{1,0:T(8,128)}) %reduce-scatter.4.cloned.1.call-update) | async-done | bytes 6416
  828.5 1.9 reshape_bitcast_fusion
  (119 shorter events, 40.7 us)
Async XLA Ops:
  7.2 73.1 %copy-start = (f32[1,1,25600]{2,1,0:T(1,128)S(1)}, f32[1,1,25600]{2,1,0:T(1,128)}, u32[]{:S(2)}) copy-start(f32[1,1,25600]{2,1,0:T(1,128)} %param.8) | copy-start | bytes 307204
  7.2 821.3 %reduce-scatter.4.cloned.1.call-start = ((), (), s32[]{:S(2)}) async-start(), calls=%async_computation.1 | async-start | bytes 13516800
  7.2 26.3 %collective-permute-start = (f32[1,25600]{1,0:T(1,128)}, f32[1,25600]{1,0:T(1,128)S(1)}, u32[]{:S(2)}, u32[]{:S(2)}) collective-permute-start(f32[1,25600]{1,0:T(1,128)} %param.9), channel_id=1, source_target_pairs={{0,1},{1,2},{2,3},{3,4},{4,5},{5,6},{6,7},{7,8},{8,9},{9,10},{10,1... | collective-permute-start | bytes 307208 | tf_op jit(solution)/shard_map/ppermute | solution.py:24
  11.7 21.8 %collective-permute-start.1 = (f32[1,25600]{1,0:T(1,128)}, f32[1,25600]{1,0:T(1,128)S(1)}, u32[]{:S(2)}, u32[]{:S(2)}) collective-permute-start(f32[1,25600]{1,0:T(1,128)} %param.9), channel_id=1, source_target_pairs={{1,0},{2,1},{3,2},{4,3},{5,4},{6,5},{7,6},{8,7},{9,8},{10,9},{11,1... | collective-permute-start | bytes 307208 | tf_op jit(solution)/shard_map/ppermute | solution.py:26
  18.3 20.6 %collective-permute-start.3 = (f32[1,2,1,25600]{3,1,2,0:T(2,128)S(1)}, f32[1,2,1,25600]{3,1,2,0:T(2,128)S(1)}, u32[]{:S(2)}, u32[]{:S(2)}) collective-permute-start(f32[1,2,1,25600]{3,1,2,0:T(2,128)S(1)} %pad_multiply_fusion.2), channel_id=1, source_target_pairs={{1,0},{2,1},{3,2},{4,3},{5,4},{6,5},{7,6},{8,7},{9,8},{10,9},{11,1... | collective-permute-start | bytes 614408 | tf_op jit(solution)/shard_map/ppermute | solution.py:26
  20.3 18.7 %collective-permute-start.2 = (f32[1,2,1,25600]{3,1,2,0:T(2,128)S(1)}, f32[1,2,1,25600]{3,1,2,0:T(2,128)S(1)}, u32[]{:S(2)}, u32[]{:S(2)}) collective-permute-start(f32[1,2,1,25600]{3,1,2,0:T(2,128)S(1)} %pad_multiply_fusion.2), channel_id=1, source_target_pairs={{0,1},{1,2},{2,3},{3,4},{4,5},{5,6},{6,7},{7,8},{8,9},{9,10},{10,1... | collective-permute-start | bytes 614408 | tf_op jit(solution)/shard_map/ppermute | solution.py:24
  41.1 7.1 collective-permute-start.5
  43.0 6.3 collective-permute-start.4
  50.7 7.8 collective-permute-start.7
  52.6 7.1 collective-permute-start.6
  60.9 7.8 collective-permute-start.9
  62.9 7.1 collective-permute-start.8
  70.0 184.8 %copy-start.1 = (s32[1,256]{1,0:T(1,128)S(1)}, s32[1,256]{1,0:T(1,128)}, u32[]{:S(2)}) copy-start(s32[1,256]{1,0:T(1,128)} %param.12) | copy-start | bytes 3076
  70.0 184.8 %copy-start.2 = (f32[2,1,256]{2,1,0:T(1,128)S(1)}, f32[2,1,256]{2,1,0:T(1,128)}, u32[]{:S(2)}) copy-start(f32[2,1,256]{2,1,0:T(1,128)} %param.14) | copy-start | bytes 6148
  70.0 184.8 %copy-start.3 = (f32[2]{0:T(128)S(1)}, f32[2]{0:T(128)}, u32[]{:S(2)}) copy-start(f32[2]{0:T(128)} %constant.91.clone) | copy-start | bytes 28
  71.2 7.8 collective-permute-start.11
  73.2 7.1 collective-permute-start.10
  272.7 17.7 %collective-permute-start.13 = (f32[1,2,1,25600]{3,1,2,0:T(2,128)S(1)}, f32[1,2,1,25600]{3,1,2,0:T(2,128)S(1)}, u32[]{:S(2)}, u32[]{:S(2)}) collective-permute-start(f32[1,2,1,25600]{3,1,2,0:T(2,128)S(1)} %bitcast_multiply_fusion.3), channel_id=1, source_target_pairs={{1,0},{2,1},{3,2},{4,3},{5,4},{6,5},{7,6},{8,7},{9,8},{10,9},{11,1... | collective-permute-start | bytes 614408 | tf_op jit(solution)/shard_map/ppermute | solution.py:26
  279.6 12.1 %collective-permute-start.12 = (f32[1,2,1,25600]{3,1,2,0:T(2,128)S(1)}, f32[1,2,1,25600]{3,1,2,0:T(2,128)S(1)}, u32[]{:S(2)}, u32[]{:S(2)}) collective-permute-start(f32[1,2,1,25600]{3,1,2,0:T(2,128)S(1)} %bitcast_multiply_fusion.3), channel_id=1, source_target_pairs={{0,1},{1,2},{2,3},{3,4},{4,5},{5,6},{6,7},{7,8},{8,9},{9,10},{10,1... | collective-permute-start | bytes 614408 | tf_op jit(solution)/shard_map/ppermute | solution.py:24
  292.9 7.8 collective-permute-start.15
  294.8 7.1 collective-permute-start.14
  303.2 14.6 %collective-permute-start.17 = (f32[1,2,1,25600]{3,1,2,0:T(2,128)S(1)}, f32[1,2,1,25600]{3,1,2,0:T(2,128)S(1)}, u32[]{:S(2)}, u32[]{:S(2)}) collective-permute-start(f32[1,2,1,25600]{3,1,2,0:T(2,128)S(1)} %get-tuple-element.6), channel_id=1, source_target_pairs={{1,0},{2,1},{3,2},{4,3},{5,4},{6,5},{7,6},{8,7},{9,8},{10,9},{11,1... | collective-permute-start | bytes 614408 | tf_op jit(solution)/shard_map/ppermute | solution.py:26
  305.1 13.9 %collective-permute-start.16 = (f32[1,2,1,25600]{3,1,2,0:T(2,128)S(1)}, f32[1,2,1,25600]{3,1,2,0:T(2,128)S(1)}, u32[]{:S(2)}, u32[]{:S(2)}) collective-permute-start(f32[1,2,1,25600]{3,1,2,0:T(2,128)S(1)} %get-tuple-element.6), channel_id=1, source_target_pairs={{0,1},{1,2},{2,3},{3,4},{4,5},{5,6},{6,7},{7,8},{8,9},{9,10},{10,1... | collective-permute-start | bytes 614408 | tf_op jit(solution)/shard_map/ppermute | solution.py:24
  320.3 7.8 collective-permute-start.19
  322.2 7.1 collective-permute-start.18
  330.6 14.5 %collective-permute-start.21 = (f32[1,2,1,25600]{3,1,2,0:T(2,128)S(1)}, f32[1,2,1,25600]{3,1,2,0:T(2,128)S(1)}, u32[]{:S(2)}, u32[]{:S(2)}) collective-permute-start(f32[1,2,1,25600]{3,1,2,0:T(2,128)S(1)} %get-tuple-element.2), channel_id=1, source_target_pairs={{1,0},{2,1},{3,2},{4,3},{5,4},{6,5},{7,6},{8,7},{9,8},{10,9},{11,1... | collective-permute-start | bytes 614408 | tf_op jit(solution)/shard_map/ppermute | solution.py:26
  332.5 13.7 %collective-permute-start.20 = (f32[1,2,1,25600]{3,1,2,0:T(2,128)S(1)}, f32[1,2,1,25600]{3,1,2,0:T(2,128)S(1)}, u32[]{:S(2)}, u32[]{:S(2)}) collective-permute-start(f32[1,2,1,25600]{3,1,2,0:T(2,128)S(1)} %get-tuple-element.2), channel_id=1, source_target_pairs={{0,1},{1,2},{2,3},{3,4},{4,5},{5,6},{6,7},{7,8},{8,9},{9,10},{10,1... | collective-permute-start | bytes 614408 | tf_op jit(solution)/shard_map/ppermute | solution.py:24
  349.8 10.0 %collective-permute-start.23 = (f32[2,2,1,25600]{3,1,2,0:T(2,128)S(1)}, f32[2,2,1,25600]{3,1,2,0:T(2,128)S(1)}, u32[]{:S(2)}, u32[]{:S(2)}) collective-permute-start(f32[2,2,1,25600]{3,1,2,0:T(2,128)S(1)} %pad_maximum_fusion), channel_id=1, source_target_pairs={{1,0},{2,1},{3,2},{4,3},{5,4},{6,5},{7,6},{8,7},{9,8},{10,9},{11,1... | collective-permute-start | bytes 1228808 | tf_op jit(solution)/shard_map/ppermute | solution.py:26
  351.7 9.3 %collective-permute-start.22 = (f32[2,2,1,25600]{3,1,2,0:T(2,128)S(1)}, f32[2,2,1,25600]{3,1,2,0:T(2,128)S(1)}, u32[]{:S(2)}, u32[]{:S(2)}) collective-permute-start(f32[2,2,1,25600]{3,1,2,0:T(2,128)S(1)} %pad_maximum_fusion), channel_id=1, source_target_pairs={{0,1},{1,2},{2,3},{3,4},{4,5},{5,6},{6,7},{7,8},{8,9},{9,10},{10,1... | collective-permute-start | bytes 1228808 | tf_op jit(solution)/shard_map/ppermute | solution.py:24
Sparse Core Ops, SparseCore 0:
  435.7 392.7 reduce-scatter.3
where the time goes:
time: 849 us; the launch traced here: 840 us
  waiting for transfers between devices  415 us (49%)
  blocking collectives  154 us (18%)
  local copies, waits for them, and re-layouts  114 us (13%)
  starting transfers between devices  102 us (12%)
  other arithmetic  38.9 us (5%)
  between operations  15.4 us (2%)
    unnamed x2, waiting for transfers between devices  393 us
    psum x1, blocking collectives, body(): readings = lax.psum(local_read, 'slab')  154 us
    unnamed x14, local copies, waits for them, and re-layouts  75.7 us
    ppermute x12, starting transfers between devices, padded_2(): lax.ppermute(tail, axis, [(i, (i + 1) % count) for i in range(ends)])  70.6 us
    ppermute x12, starting transfers between devices, padded_2(): lax.ppermute(head, axis, [((i + 1) % count, i) for i in range(ends)])  31.6 us
  transfers between devices with their start and end apart: 25, of which 21 were waited for; matrix products, arithmetic and copies ran while one was open for 3% of the time, Pallas kernels for 0%

commit v1 on v0

v1 whole, which is shorter than its diff:
```python
import jax
import jax.numpy as jnp
from jax import lax
from jax.experimental import pallas as pl
from jax.experimental.pallas import tpu as pltpu
from jax.sharding import PartitionSpec as P

NY = 160
SWEEPS = 6
NDET = 512
PAIRS = 256
SLABS = 16
OWN = 10
HALO = 6
SLOT = 32
LANES = 128
MESH = pl.DeviceIdType.MESH
F32 = jnp.float32
BF16 = jnp.bfloat16

spectrum_low = 0.02
spectrum_high = 25.0
frequency_shift = 0.3


def chebyshev_terms():
    theta = (spectrum_high + spectrum_low) / 2.0
    delta = (spectrum_high - spectrum_low) / 2.0
    sigma = theta / delta
    rho = 1.0 / sigma
    keeps = []
    pushes = []
    for sweep in range(SWEEPS - 1):
        rho_new = 1.0 / (2.0 * sigma - rho)
        keeps.append(rho_new * rho)
        pushes.append(2.0 * rho_new / delta)
        rho = rho_new
    return (1.0 / theta, keeps, pushes)


def parts_of(value):
    high = value.astype(BF16)
    rest = value - high.astype(F32)
    middle = rest.astype(BF16)
    low = (rest - middle.astype(F32)).astype(BF16)
    return (high, middle, low)


def dot_parts(lhs_parts, rhs_parts, dims):
    total = None
    for lhs in lhs_parts:
        for rhs in rhs_parts:
            term = lax.dot_general(lhs, rhs, (dims, ((), ())), preferred_element_type=F32)
            total = term if total is None else total + term
    return total


def pick(table, index):
    value = jnp.float32(table[0])
    for which in range(1, len(table)):
        value = jnp.where(index == which, jnp.float32(table[which]), value)
    return value


def kernel(
    count_ref, source_ref, kappa_ref, absorb_ref, cell_ref, pair_ref, measured_ref,
    out_abs_ref, out_dif_ref,
    plain, half, send, recv, coef, direc, resid, field, grads,
    place, lane_hot, pair_hot, reads, ysend, yrecv, fsend, frecv,
    a_send, a_recv, r_send, r_recv, y_send, y_recv, f_send, f_recv,
):
    src = lax.axis_index("src")
    slab = lax.axis_index("slab")
    my_y = src // 8
    my_zlo = src % 8

    def is_me(dev):
        return (dev[0] == src) & (dev[1] == slab)

    slab_peers = [(src, lax.rem(slab + j, SLABS)) for j in range(1, SLABS)]
    y_peers = [(lax.rem(my_y + j, 4) * 8 + my_zlo, slab) for j in range(1, 4)]
    final_to = [[(2 * slab + h, 4 * my_y + t) for h in range(2)] for t in range(4)]
    final_from = [((slab // 4) * 8 + m, src // 2) for m in range(8)]

    barrier = pltpu.get_barrier_semaphore()
    for dev in slab_peers + y_peers:
        pl.semaphore_signal(barrier, inc=1, device_id=dev, device_id_type=MESH)
    for dev in final_from:
        mine = is_me(dev)

        @pl.when(jnp.logical_not(mine))
        def _():
            pl.semaphore_signal(barrier, inc=1, device_id=dev, device_id_type=MESH)

    to_self = jnp.where((src // 8 == slab // 4) & (slab == src // 2), 1, 0)

    lane = lax.broadcasted_iota(jnp.int32, (SLOT, LANES), 1)
    flat = lax.broadcasted_iota(jnp.int32, (SLOT, LANES), 0) * LANES + lane
    row = ((flat >> 5) * 205) >> 10
    col = flat - row * NY
    real_row = row + (OWN * slab - HALO)
    row_in = (real_row >= 0) & (real_row < 160)
    xp_in = (row_in & (real_row < 159)).astype(F32)
    xm_in = (row_in & (real_row > 0)).astype(F32)
    yp_in = (col < NY - 1).astype(F32)
    ym_in = (col > 0).astype(F32)

    def x_plus(ref, base):
        near, far = ref[pl.ds(base + 1, SLOT), :], ref[pl.ds(base + 2, SLOT), :]
        return pltpu.roll(jnp.where(lane >= 32, near, far), 96, 1)

    def x_minus(ref, base):
        near, far = ref[pl.ds(base - 1, SLOT), :], ref[pl.ds(base - 2, SLOT), :]
        return pltpu.roll(jnp.where(lane < 96, near, far), 32, 1)

    def y_plus(ref, base, here):
        return pltpu.roll(jnp.where(lane >= 1, here, ref[pl.ds(base + 1, SLOT), :]), 127, 1)

    def y_minus(ref, base, here):
        return pltpu.roll(jnp.where(lane < 127, here, ref[pl.ds(base - 1, SLOT), :]), 1, 1)

    def at(p):
        return pl.multiple_of(p * SLOT, SLOT)

    tall = plain.shape[1]
    rows_in = kappa_ref.shape[0]
    for which, ref in enumerate((kappa_ref, absorb_ref, source_ref)):
        plane = ref[...]
        plain[which, pl.ds(0, rows_in), :] = plane
        plain[which, pl.ds(rows_in, tall - rows_in), :] = jnp.zeros((tall - rows_in, LANES), F32)
        half[which, pl.ds(0, 8), :] = jnp.zeros((8, LANES), F32)
        half[which, pl.ds(8, rows_in), :] = pltpu.roll(plane, 64, 1)
        half[which, pl.ds(8 + rows_in, tall - rows_in - 8), :] = jnp.zeros((tall - rows_in - 8, LANES), F32)
        for m in range(8):
            send[2 * m, which] = jnp.where(
                lane < 64, half[which, pl.ds(25 * m, SLOT), :], half[which, pl.ds(25 * m + 1, SLOT), :]
            )
            send[2 * m + 1, which] = plain[which, pl.ds(25 * m + 5, SLOT), :]

    pl.semaphore_wait(barrier, 15 + 3 + 8 - to_self)
    copies = []
    for j, dev in enumerate(slab_peers):
        copy = pltpu.make_async_remote_copy(
            src_ref=send.at[dev[1]],
            dst_ref=recv.at[:, pl.ds(at(slab + 1), SLOT), :],
            send_sem=a_send.at[j],
            recv_sem=a_recv.at[j],
            device_id=dev,
            device_id_type=MESH,
        )
        copy.start()
        copies.append(copy)

    guard = jnp.zeros((SLOT, LANES), F32)
    last = (SLABS + 1) * SLOT
    for start in (0, last):
        recv[0, pl.ds(start, SLOT), :] = guard
        for a in range(2):
            for b in range(2):
                direc[a, b, pl.ds(start, SLOT), :] = guard
                field[a, b, pl.ds(start, SLOT), :] = guard
    recv[:, pl.ds(at(slab + 1), SLOT), :] = send[slab]

    cell = cell_ref[...]
    det_z = ((cell >> 10) * 1311) >> 15
    in_plane = cell - det_z * 25600
    det_x = ((in_plane >> 5) * 6554) >> 15
    det_y = in_plane - det_x * NY
    det_row = det_x - (OWN * slab - HALO)
    in_window = (det_row >= 0) & (det_row < OWN + 2 * HALO)
    owned = ((det_row >= HALO) & (det_row < HALO + OWN)).astype(F32)
    spot = det_row * NY + det_y
    det_sub = jnp.where(in_window, det_z * SLOT + (spot >> 7), -1)
    det_lane = spot & 127

    @pl.loop(0, SLABS)
    def _(p):
        subs = lax.broadcasted_iota(jnp.int32, (SLOT, NDET), 0) + p * SLOT
        place[pl.ds(at(p), SLOT), :] = (subs == det_sub).astype(F32).astype(BF16)

    lane_hot[...] = (lax.broadcasted_iota(jnp.int32, (LANES, NDET), 0) == det_lane).astype(F32)
    pair_hot[...] = (
        lax.broadcasted_iota(jnp.int32, (NDET, PAIRS), 0) == pair_ref[...]
    ).astype(F32).astype(BF16)

    for copy in copies:
        copy.wait()

    first, keeps, pushes = chebyshev_terms()
    kappa, absorb, source = recv.at[0], recv.at[1], recv.at[2]

    @pl.loop(0, SLABS)
    def _(p):
        base, here = at(p + 1), at(p)
        k = kappa[pl.ds(base, SLOT), :]
        diagonal = absorb[pl.ds(base, SLOT), :]
        beside = (
            (x_plus(kappa, base), xp_in),
            (x_minus(kappa, base), xm_in),
            (y_plus(kappa, base, k) * yp_in, yp_in),
            (y_minus(kappa, base, k) * ym_in, ym_in),
            (kappa[pl.ds(base + SLOT, SLOT), :], jnp.where(p < SLABS - 1, 1.0, 0.0).astype(F32)),
            (kappa[pl.ds(base - SLOT, SLOT), :], jnp.where(p > 0, 1.0, 0.0).astype(F32)),
        )
        for which, (side, inside) in enumerate(beside):
            face = (k + side) * 0.5
            diagonal = diagonal + face
            coef[which, pl.ds(here, SLOT), :] = face * inside
        coef[6, pl.ds(here, SLOT), :] = diagonal
        b = source[pl.ds(base, SLOT), :]
        resid[0, pl.ds(here, SLOT), :] = b
        resid[1, pl.ds(here, SLOT), :] = jnp.zeros_like(b)
        direc[0, 0, pl.ds(base, SLOT), :] = b * first
        direc[0, 1, pl.ds(base, SLOT), :] = jnp.zeros_like(b)
        field[0, 0, pl.ds(base, SLOT), :] = b * first
        field[0, 1, pl.ds(base, SLOT), :] = jnp.zeros_like(b)

    def solve(out):
        @pl.loop(0, SWEEPS - 1)
        def _(sweep):
            keep, push = pick(keeps, sweep), pick(pushes, sweep)
            now, later = sweep % 2, (sweep + 1) % 2

            @pl.loop(0, SLABS)
            def _(p):
                base, here = at(p + 1), at(p)
                cs = [coef[which, pl.ds(here, SLOT), :] for which in range(7)]
                ds = [direc[now, c, pl.ds(base, SLOT), :] for c in range(2)]
                turned = (-ds[1], ds[0])
                for c in range(2):
                    ref = direc.at[now, c]
                    off = (
                        cs[0] * x_plus(ref, base)
                        + cs[1] * x_minus(ref, base)
                        + cs[2] * y_plus(ref, base, ds[c])
                        + cs[3] * y_minus(ref, base, ds[c])
                        + cs[4] * ref[pl.ds(base + SLOT, SLOT), :]
                        + cs[5] * ref[pl.ds(base - SLOT, SLOT), :]
                    )
                    applied = cs[6] * ds[c] - off + frequency_shift * turned[c]
                    left = resid[c, pl.ds(here, SLOT), :] - applied
                    resid[c, pl.ds(here, SLOT), :] = left
                    new = keep * ds[c] + push * left
                    direc[later, c, pl.ds(base, SLOT), :] = new
                    field[out, c, pl.ds(base, SLOT), :] = field[out, c, pl.ds(base, SLOT), :] + new

    solve(0)

    whole = pl.ds(SLOT, SLABS * SLOT)
    for c in range(2):
        spread = dot_parts(parts_of(field[0, c, whole, :]), (place[...],), ((0,), (0,)))
        reads[slab, pl.ds(c, 1), :] = jnp.sum(spread * lane_hot[...], axis=0, keepdims=True) * owned
    copies = []
    for j, dev in enumerate(slab_peers):
        copy = pltpu.make_async_remote_copy(
            src_ref=reads.at[slab],
            dst_ref=reads.at[slab],
            send_sem=r_send.at[j],
            recv_sem=r_recv.at[j],
            device_id=dev,
            device_id_type=MESH,
        )
        copy.start()
        copies.append(copy)
    for copy in copies:
        copy.wait()
    readings = jnp.sum(reads[...], axis=0)
    wide = jnp.concatenate([readings, jnp.zeros((6, NDET), F32)], axis=0)
    model = dot_parts(parts_of(wide), (pair_hot[...],), ((1,), (0,)))
    active = (lax.broadcasted_iota(jnp.int32, (1, PAIRS), 1) < count_ref[0]).astype(F32)
    conj = jnp.concatenate(
        [
            (model[0:1] - measured_ref[0]) * active,
            (measured_ref[1] - model[1:2]) * active,
            jnp.zeros((6, PAIRS), F32),
        ],
        axis=0,
    )
    weights = dot_parts(parts_of(conj), (pair_hot[...],), ((1,), (1,)))
    for c in range(2):
        hot = lane_hot[...]
        pieces = [(hot * part.astype(F32)).astype(BF16) for part in parts_of(weights[c : c + 1])]
        right = dot_parts((place[...],), pieces, ((1,), (1,)))
        resid[c] = right
        direc[0, c, whole, :] = right * first
        field[1, c, whole, :] = right * first

    solve(1)

    @pl.loop(0, SLABS)
    def _(p):
        base = at(p + 1)
        refs = [[field.at[a, c] for c in range(2)] for a in range(2)]
        here = [[refs[a][c][pl.ds(base, SLOT), :] for c in range(2)] for a in range(2)]
        sides = (
            x_plus,
            x_minus,
            lambda ref, b: y_plus(ref, b, ref[pl.ds(b, SLOT), :]) * yp_in,
            lambda ref, b: y_minus(ref, b, ref[pl.ds(b, SLOT), :]) * ym_in,
            lambda ref, b: ref[pl.ds(b + SLOT, SLOT), :],
            lambda ref, b: ref[pl.ds(b - SLOT, SLOT), :],
        )
        total = jnp.zeros((SLOT, LANES), F32)
        for side in sides:
            gap = [[here[a][c] - side(refs[a][c], base) for c in range(2)] for a in range(2)]
            total = total + gap[0][0] * gap[1][0] - gap[0][1] * gap[1][1]
        grads[0] = here[0][1] * here[1][1] - here[0][0] * here[1][0]
        grads[1] = -0.5 * total
        for out in range(2):
            low, high = grads[out, pl.ds(7, 16), :], grads[out, pl.ds(8, 16), :]
            ysend[p, out] = pltpu.roll(jnp.where(lane[0:16] >= 64, low, high), 64, 1)

    copies = []
    for j, dev in enumerate(y_peers):
        copy = pltpu.make_async_remote_copy(
            src_ref=ysend.at[pl.ds((dev[0] // 8) * 4, 4)],
            dst_ref=yrecv.at[j],
            send_sem=y_send.at[j],
            recv_sem=y_recv.at[j],
            device_id=dev,
            device_id_type=MESH,
        )
        copy.start()
        copies.append(copy)
    for copy in copies:
        copy.wait()
    for t in range(4):
        for out in range(2):
            total = ysend[my_y * 4 + t, out] + yrecv[0, t, out] + yrecv[1, t, out] + yrecv[2, t, out]
            fsend[t, 0, out] = total[0:8]
            grads[out, pl.ds(0, 16), :] = total
            low, high = grads[out, pl.ds(6, 8), :], grads[out, pl.ds(7, 8), :]
            fsend[t, 1, out] = pltpu.roll(jnp.where(lane[0:8] >= 32, low, high), 96, 1)

    def final_copy(t, h):
        return pltpu.make_async_remote_copy(
            src_ref=fsend.at[t, h],
            dst_ref=frecv.at[my_zlo],
            send_sem=f_send.at[2 * t + h],
            recv_sem=f_recv.at[my_zlo],
            device_id=final_to[t][h],
            device_id_type=MESH,
        )

    for t in range(4):
        for h in range(2):
            mine = is_me(final_to[t][h])

            @pl.when(jnp.logical_not(mine))
            def _():
                final_copy(t, h).start()

            @pl.when(mine)
            def _():
                pltpu.make_async_copy(fsend.at[t, h], frecv.at[my_zlo], f_recv.at[my_zlo]).start()

    for m in range(8):
        pltpu.make_async_copy(frecv.at[m], frecv.at[m], f_recv.at[m]).wait()
    for out, out_ref in enumerate((out_abs_ref, out_dif_ref)):
        total = frecv[0, out]
        for m in range(1, 8):
            total = total + frecv[m, out]
        for k in range(6):
            out_ref[0:1, pl.ds(128 * k, 128)] = total[k : k + 1]
        out_ref[0:1, pl.ds(768, 32)] = total[6:7, 0:32]
    for t in range(4):
        for h in range(2):

            @pl.when(jnp.logical_not(is_me(final_to[t][h])))
            def _():
                final_copy(t, h).wait_send()


def body(source_field, kappa, absorb, det_cell, pair_det, pair_count, measured):
    tall = 216
    vmem = pl.BlockSpec(memory_space=pltpu.VMEM)
    stacked = (SLABS + 2) * SLOT
    flat = SLABS * SLOT
    out = jax.ShapeDtypeStruct((1, 800), F32)
    dma = pltpu.SemaphoreType.DMA
    return pl.pallas_call(
        kernel,
        out_shape=(out, out),
        in_specs=[pl.BlockSpec(memory_space=pltpu.SMEM)] + [vmem] * 6,
        out_specs=(vmem, vmem),
        scratch_shapes=[
            pltpu.VMEM((3, tall, LANES), F32),
            pltpu.VMEM((3, tall, LANES), F32),
            pltpu.VMEM((SLABS, 3, SLOT, LANES), F32),
            pltpu.VMEM((3, stacked, LANES), F32),
            pltpu.VMEM((7, flat, LANES), F32),
            pltpu.VMEM((2, 2, stacked, LANES), F32),
            pltpu.VMEM((2, flat, LANES), F32),
            pltpu.VMEM((2, 2, stacked, LANES), F32),
            pltpu.VMEM((2, SLOT, LANES), F32),
            pltpu.VMEM((flat, NDET), BF16),
            pltpu.VMEM((LANES, NDET), F32),
            pltpu.VMEM((NDET, PAIRS), BF16),
            pltpu.VMEM((SLABS, 2, NDET), F32),
            pltpu.VMEM((SLABS, 2, 16, LANES), F32),
            pltpu.VMEM((3, 4, 2, 16, LANES), F32),
            pltpu.VMEM((4, 2, 2, 8, LANES), F32),
            pltpu.VMEM((8, 2, 8, LANES), F32),
            dma((15,)), dma((15,)), dma((15,)), dma((15,)),
            dma((3,)), dma((3,)), dma((8,)), dma((8,)),
        ],
        compiler_params=pltpu.CompilerParams(
            collective_id=0, has_side_effects=True, vmem_limit_bytes=40 * 1024 * 1024
        ),
    )(
        pair_count,
        source_field.reshape(200, LANES),
        kappa.reshape(200, LANES),
        absorb.reshape(200, LANES),
        det_cell.reshape(1, NDET),
        pair_det,
        measured,
    )


def solution(mesh):
    placed = (
        P("src", "slab", None),
        P("slab", None),
        P("slab", None),
        P(),
        P("src", None),
        P("src"),
        P(None, "src", None),
    )
    return jax.shard_map(
        body,
        mesh=mesh,
        in_specs=placed,
        out_specs=(P("slab", "src"), P("slab", "src")),
        check_vma=False,
    )
```

time: 849 us -> 126 us (0.15)
  waiting for transfers between devices: 415 us -> 0 us
  blocking collectives: 154 us -> 0 us
  Pallas kernels: 0 us -> 119 us
  local copies, waits for them, and re-layouts: 114 us -> 4.53 us
  starting transfers between devices: 102 us -> 0 us
  other arithmetic: 38.9 us -> 0 us
  between operations: 15.4 us -> 1.31 us
    unnamed x2 -> x0, waiting for transfers between devices: 393 us -> none
    psum x1 -> x0, blocking collectives: 154 us -> none  [body(): readings = lax.psum(local_read, 'slab')]
    pallas_call x0 -> x1, Pallas kernels: none -> 119 us  [body(): pl.pallas_call(kernel, out_shape=(out, out), in_specs=[pl.BlockSpec(memor...]
    ppermute x24 -> x0, starting transfers between devices: 102 us -> none  [the longest x12 70.6 us: padded_2(): lax.ppermute(tail, axis, [(i, (i + 1) % count) for i in range(ends)])]
    unnamed x14, local copies, waits for them, and re-layouts: 75.7 us -> 4.53 us
    add x13 -> x0, other arithmetic: 22.3 us -> none  [the longest x8 9.19 us: solve(): direction = keeps[sweep] * direction + pushes[sweep] * residual_field]
    ppermute x24 -> x0, waiting for transfers between devices: 22.3 us -> none  [the longest x12 11.8 us: padded_2(): lax.ppermute(tail, axis, [(i, (i + 1) % count) for i in range(ends)])]
    slice x53 -> x0, local copies, waits for them, and re-layouts: 13.6 us -> none  [the longest x40 7.02 us: apply_operator(): jnp.roll(field, shifts[which][0], axis=3)]
  transfers between devices with their start and end apart: 25 -> 0, of which waited for: 21 -> 0; matrix products, arithmetic and copies ran while one was open for 3% -> 0% of each run, Pallas kernels for 0% -> 0%
where the time goes in v1:
time: 126 us; the launch traced here: 125 us
  Pallas kernels  119 us (94%)
  local copies, waits for them, and re-layouts  4.53 us (4%)
  between operations  1.31 us (1%)
    pallas_call x1, Pallas kernels, body(): pl.pallas_call(kernel, out_shape=(out, out), in_specs=[pl.BlockSpec(memor...  119 us
    unnamed x14, local copies, waits for them, and re-layouts  4.53 us

profile of v1, /device:TPU:1, one launch (start us, length us, event | category | flops | bytes accessed | tf_op | source)
XLA Modules:
  0.0 125.3 jit_solution(13844851085858448431)
XLA Ops:
  1.3 0.0 copy-start.4
  1.3 0.0 copy-start.3
  1.3 0.0 copy-start.5
  1.3 0.7 copy-done.4
  2.0 0.0 copy-done.3
  2.0 0.0 copy-done.5
  2.0 0.0 copy-start
  2.0 0.9 copy-done
  2.9 0.0 copy-start.1
  2.9 0.9 copy-done.1
  3.8 0.0 copy-start.2
  3.8 0.9 copy-done.2
  4.7 119.5 %shard_map.86 = (f32[1,800]{1,0:T(1,128)S(1)}, f32[1,800]{1,0:T(1,128)S(1)}) custom-call(s32[1]{0:T(128)S(6)} %copy.11.count_ref, f32[200,128]{1,0:T(8,128)S(1)} %bitcast.4, f32[200,128]{1,0:T(8,128)S(1)} %bitcast.5, f32[200,128]{1,0:T(8,128)S(1)} %bitcast.6, s32[1,512]{1,0:T(1,128)S(1)} %bitcast.7, s32[1,256]{1,0:T(1,128)S(1)} %copy-done.5, ...), custom_call_target="tpu_custom_call" | custom-call | tf_op jit(solution)/shard_map/pallas_call | solution.py:381
  124.1 0.6 copy.12
  124.7 0.6 copy.13
Async XLA Ops:
  1.3 0.7 copy-start.4
  1.3 0.7 copy-start.3
  1.3 0.7 copy-start.5
  2.0 0.9 copy-start
  2.9 0.9 copy-start.1
  3.8 0.9 copy-start.2

commit v2 on v1

v2 whole, which is shorter than its diff:
```python
import jax
import jax.numpy as jnp
from jax import lax
from jax.experimental import pallas as pl
from jax.experimental.pallas import tpu as pltpu
from jax.sharding import PartitionSpec as P

NY = 160
SWEEPS = 6
NDET = 512
PAIRS = 256
SLABS = 16
OWN = 10
HALO = 6
SLOT = 32
LANES = 128
MESH = pl.DeviceIdType.MESH
F32 = jnp.float32
BF16 = jnp.bfloat16

spectrum_low = 0.02
spectrum_high = 25.0
frequency_shift = 0.3


def chebyshev_terms():
    theta = (spectrum_high + spectrum_low) / 2.0
    delta = (spectrum_high - spectrum_low) / 2.0
    sigma = theta / delta
    rho = 1.0 / sigma
    keeps = []
    pushes = []
    for sweep in range(SWEEPS - 1):
        rho_new = 1.0 / (2.0 * sigma - rho)
        keeps.append(rho_new * rho)
        pushes.append(2.0 * rho_new / delta)
        rho = rho_new
    return (1.0 / theta, keeps, pushes)


def parts_of(value):
    high = value.astype(BF16)
    rest = value - high.astype(F32)
    middle = rest.astype(BF16)
    low = (rest - middle.astype(F32)).astype(BF16)
    return (high, middle, low)


def dot_parts(lhs_parts, rhs_parts, dims):
    total = None
    for lhs in lhs_parts:
        for rhs in rhs_parts:
            term = lax.dot_general(lhs, rhs, (dims, ((), ())), preferred_element_type=F32)
            total = term if total is None else total + term
    return total


def pick(table, index):
    value = jnp.float32(table[0])
    for which in range(1, len(table)):
        value = jnp.where(index == which, jnp.float32(table[which]), value)
    return value


def kernel(
    count_ref, source_ref, kappa_ref, absorb_ref, cell_ref, pair_ref, measured_ref,
    out_abs_ref, out_dif_ref,
    plain, half_lane, send, coef_recv, source, kappa, coef, direc_a, direc_b, resid, field, grads,
    place, lane_hot, pair_hot, pair_send, pair_recv, reads, ysend, yrecv, fsend, frecv,
    s_send, s_recv, k_send, k_recv, o_send, o_recv, g_send, g_recv, p_send, p_recv,
    r_send, r_recv, y_send, y_recv, f_send, f_recv,
):
    src = lax.axis_index("src")
    slab = lax.axis_index("slab")
    my_y = src // 8
    my_z = (slab // 8) * 8 + src % 8
    my_spot = slab % 8
    parity = my_z % 2
    pair_z = my_z - parity
    group = parity * 8 + my_spot
    solved = jnp.where((pair_z >= 4) & (pair_z <= 10), pair_z - 4, lax.rem(pair_z + 5, 16))
    own_zlo = src % 8
    goal_z = jnp.where(own_zlo % 2 == 0, own_zlo + 4, lax.rem(own_zlo + 11, 16))
    other_half = 1 - my_z // 8
    swap_z = jnp.where(src % 8 < 4, lax.rem(my_z + 12, 16), lax.rem(my_z + 4, 16))

    def device(y, z, spot):
        return (y * 8 + lax.rem(z, 8), (z // 8) * 8 + spot)

    def is_me(dev):
        return (dev[0] == src) & (dev[1] == slab)

    source_to = [device(my_y, goal_z + i // 8, i % 8) for i in range(SLABS)]
    source_from = [(my_y * 8 + solved, p) for p in range(SLABS)]
    near = [device(my_y, my_z, lax.rem(my_spot + j, 8)) for j in range(1, 8)]
    beyond = [device(my_y, swap_z, spot) for spot in range(8)]
    twin = [device(my_y, pair_z + 1 - parity, spot) for spot in range(8)]
    y_peers = [(lax.rem(my_y + j, 4) * 8 + src % 8, slab) for j in range(1, 4)]
    final_to = [[(2 * group + h, 4 * my_y + t) for h in range(2)] for t in range(4)]
    final_from = [device(slab // 4, 2 * m + src // 16, (src // 2) % 8) for m in range(8)]

    barrier = pltpu.get_barrier_semaphore()
    for dev in source_from + near + beyond + twin + y_peers:
        pl.semaphore_signal(barrier, inc=1, device_id=dev, device_id_type=MESH)
    to_self = jnp.int32(0)
    for dev in final_from:
        to_self = to_self + jnp.where(is_me(dev), 1, 0)

        @pl.when(jnp.logical_not(is_me(dev)))
        def _():
            pl.semaphore_signal(barrier, inc=1, device_id=dev, device_id_type=MESH)

    lane = lax.broadcasted_iota(jnp.int32, (SLOT, LANES), 1)
    flat = lax.broadcasted_iota(jnp.int32, (SLOT, LANES), 0) * LANES + lane
    row = ((flat >> 5) * 205) >> 10
    col = flat - row * NY
    real_row = row + (OWN * group - HALO)
    row_in = (real_row >= 0) & (real_row < 160)
    xp_in = (row_in & (real_row < 159)).astype(F32)
    xm_in = (row_in & (real_row > 0)).astype(F32)
    yp_in = (col < NY - 1).astype(F32)
    ym_in = (col > 0).astype(F32)

    def x_plus(ref, base):
        near, far = ref[pl.ds(base + 1, SLOT), :], ref[pl.ds(base + 2, SLOT), :]
        return pltpu.roll(jnp.where(lane >= 32, near, far), 96, 1)

    def x_minus(ref, base):
        near, far = ref[pl.ds(base - 1, SLOT), :], ref[pl.ds(base - 2, SLOT), :]
        return pltpu.roll(jnp.where(lane < 96, near, far), 32, 1)

    def y_plus(ref, base, here):
        return pltpu.roll(jnp.where(lane >= 1, here, ref[pl.ds(base + 1, SLOT), :]), 127, 1)

    def y_minus(ref, base, here):
        return pltpu.roll(jnp.where(lane < 127, here, ref[pl.ds(base - 1, SLOT), :]), 1, 1)

    def at(p):
        return pl.multiple_of(p * SLOT, SLOT)

    tall = plain.shape[1]
    rows_in = kappa_ref.shape[0]
    for which, ref in enumerate((kappa_ref, absorb_ref, source_ref)):
        plane = ref[...]
        plain[which, pl.ds(0, rows_in), :] = plane
        plain[which, pl.ds(rows_in, tall - rows_in), :] = jnp.zeros((tall - rows_in, LANES), F32)
        half_lane[which, pl.ds(0, 8), :] = jnp.zeros((8, LANES), F32)
        half_lane[which, pl.ds(8, rows_in), :] = pltpu.roll(plane, 64, 1)
        half_lane[which, pl.ds(8 + rows_in, tall - rows_in - 8), :] = jnp.zeros((tall - rows_in - 8, LANES), F32)
        for m in range(8):
            send[2 * m, which] = jnp.where(
                lane < 64, half_lane[which, pl.ds(25 * m, SLOT), :], half_lane[which, pl.ds(25 * m + 1, SLOT), :]
            )
            send[2 * m + 1, which] = plain[which, pl.ds(25 * m + 5, SLOT), :]

    active = (lax.broadcasted_iota(jnp.int32, (1, PAIRS), 1) < count_ref[0]).astype(F32)
    pair_send[...] = jnp.concatenate(
        [pair_ref[...].astype(F32), measured_ref[0], measured_ref[1], active, jnp.zeros((4, PAIRS), F32)],
        axis=0,
    )

    def remote(src_ref, dst_ref, send_sem, recv_sem, dev):
        copy = pltpu.make_async_remote_copy(
            src_ref=src_ref, dst_ref=dst_ref, send_sem=send_sem, recv_sem=recv_sem,
            device_id=dev, device_id_type=MESH,
        )
        copy.start()
        return copy

    def arrived(ref, sem):
        pltpu.make_async_copy(ref, ref, sem).wait()

    strip = pl.ds(pl.multiple_of(8 * my_y, 8), 8)
    two = pl.ds(0, 2)
    pl.semaphore_wait(barrier, 16 + 7 + 8 + 8 + 3 + 8 - to_self)
    sent = []
    for spot, dev in enumerate(beyond):
        sent.append(remote(
            send.at[parity * 8 + spot, two, strip, :], coef_recv.at[:, slab, strip, :],
            o_send.at[spot], o_recv.at[my_spot], dev,
        ))
    for i, dev in enumerate(source_to):
        sent.append(remote(send.at[i, 2], source.at[slab], s_send.at[i], s_recv.at[slab], dev))
    close = []
    for j, dev in enumerate(near):
        close.append(remote(
            send.at[parity * 8 + dev[1] % 8, two], coef_recv.at[:, slab], k_send.at[j], k_recv.at[j], dev
        ))
    sent.append(remote(
        pair_send, pair_recv, p_send.at[0], p_recv.at[0],
        device(my_y, goal_z + slab // 8, slab % 8),
    ))

    guard = jnp.zeros((SLOT, LANES), F32)
    last = (SLABS + 1) * SLOT
    for start in (0, last):
        kappa[pl.ds(start, SLOT), :] = guard
        for c in range(2):
            direc_a[c, pl.ds(start, SLOT), :] = guard
            direc_b[c, pl.ds(start, SLOT), :] = guard
            for a in range(2):
                field[a, c, pl.ds(start, SLOT), :] = guard
    for a in range(2):
        coef_recv[a, slab] = send[group, a]

    cell = cell_ref[...]
    det_z = ((cell >> 10) * 1311) >> 15
    in_plane = cell - det_z * 25600
    det_x = ((in_plane >> 5) * 6554) >> 15
    det_y = in_plane - det_x * NY
    det_row = det_x - (OWN * group - HALO)
    in_window = (det_row >= 0) & (det_row < OWN + 2 * HALO)
    owned = ((det_row >= HALO) & (det_row < HALO + OWN)).astype(F32)
    spot = det_row * NY + det_y
    det_sub = jnp.where(in_window, det_z * SLOT + (spot >> 7), -1)
    det_lane = spot & 127

    @pl.loop(0, SLABS)
    def _(p):
        subs = lax.broadcasted_iota(jnp.int32, (SLOT, NDET), 0) + p * SLOT
        place[pl.ds(at(p), SLOT), :] = (subs == det_sub).astype(F32).astype(BF16)

    lane_hot[...] = (lax.broadcasted_iota(jnp.int32, (LANES, NDET), 0) == det_lane).astype(F32)
    for spot in range(8):
        arrived(coef_recv.at[:, other_half * 8 + spot, strip, :], o_recv.at[spot])
    eight = pl.ds(pl.multiple_of(other_half * 8, 8), 8)
    strips = coef_recv.at[:, eight, strip, :]
    across = [remote(strips, strips, g_send.at[j], g_recv.at[j], dev) for j, dev in enumerate(y_peers)]
    for copy in close:
        copy.wait()
    for p in range(SLABS):
        arrived(source.at[p], s_recv.at[p])
    for copy in across:
        copy.wait()

    first, keeps, pushes = chebyshev_terms()

    @pl.loop(0, SLABS, unroll=4)
    def _(p):
        kappa[pl.ds(at(p + 1), SLOT), :] = coef_recv[0, p]

    @pl.loop(0, SLABS, unroll=4)
    def _(p):
        base, here = at(p + 1), at(p)
        k = kappa[pl.ds(base, SLOT), :]
        diagonal = coef_recv[1, p]
        beside = (
            (x_plus(kappa, base), xp_in),
            (x_minus(kappa, base), xm_in),
            (y_plus(kappa, base, k) * yp_in, yp_in),
            (y_minus(kappa, base, k) * ym_in, ym_in),
            (kappa[pl.ds(base + SLOT, SLOT), :], jnp.where(p < SLABS - 1, 1.0, 0.0).astype(F32)),
            (kappa[pl.ds(base - SLOT, SLOT), :], jnp.where(p > 0, 1.0, 0.0).astype(F32)),
        )
        for which, (side, inside) in enumerate(beside):
            face = (k + side) * 0.5
            diagonal = diagonal + face
            coef[which, pl.ds(here, SLOT), :] = face * inside
        coef[6, pl.ds(here, SLOT), :] = diagonal
        b = source[p]
        resid[0, pl.ds(here, SLOT), :] = b
        resid[1, pl.ds(here, SLOT), :] = jnp.zeros_like(b)
        direc_a[0, pl.ds(base, SLOT), :] = b * first
        direc_a[1, pl.ds(base, SLOT), :] = jnp.zeros_like(b)
        field[0, 0, pl.ds(base, SLOT), :] = b * first
        field[0, 1, pl.ds(base, SLOT), :] = jnp.zeros_like(b)

    size = 2 * SLOT
    lane2 = lax.broadcasted_iota(jnp.int32, (size, LANES), 1)

    def solve(out):
        for sweep in range(SWEEPS - 1):
            keep, push = keeps[sweep], pushes[sweep]
            now, later = (direc_a, direc_b) if sweep % 2 == 0 else (direc_b, direc_a)

            @pl.loop(0, SLABS // 2, unroll=8)
            def _(q):
                here, base = pl.multiple_of(q * size, size), pl.multiple_of(q * size + SLOT, SLOT)
                cs = [coef[which, pl.ds(here, size), :] for which in range(7)]
                ds = [now[c, pl.ds(base, size), :] for c in range(2)]
                turned = (-ds[1], ds[0])
                for c in range(2):

                    def shifted(amount):
                        return now[c, pl.ds(base + amount, size), :]

                    up, down = shifted(1), shifted(-1)
                    off = (
                        cs[0] * pltpu.roll(jnp.where(lane2 >= 32, up, shifted(2)), 96, 1)
                        + cs[1] * pltpu.roll(jnp.where(lane2 < 96, down, shifted(-2)), 32, 1)
                        + cs[2] * pltpu.roll(jnp.where(lane2 >= 1, ds[c], up), 127, 1)
                        + cs[3] * pltpu.roll(jnp.where(lane2 < 127, ds[c], down), 1, 1)
                        + cs[4] * shifted(SLOT)
                        + cs[5] * shifted(-SLOT)
                    )
                    applied = cs[6] * ds[c] - off + frequency_shift * turned[c]
                    left = resid[c, pl.ds(here, size), :] - applied
                    resid[c, pl.ds(here, size), :] = left
                    new = keep * ds[c] + push * left
                    later[c, pl.ds(base, size), :] = new
                    field[out, c, pl.ds(base, size), :] = field[out, c, pl.ds(base, size), :] + new

    solve(0)

    whole = pl.ds(SLOT, SLABS * SLOT)
    for c in range(2):
        spread = dot_parts(parts_of(field[0, c, whole, :]), (place[...],), ((0,), (0,)))
        reads[group, pl.ds(c, 1), :] = jnp.sum(spread * lane_hot[...], axis=0, keepdims=True) * owned
    mine = reads.at[group]
    for j, dev in enumerate(near):
        sent.append(remote(mine, mine, r_send.at[j], r_recv.at[group], dev))
    for spot, dev in enumerate(twin):
        sent.append(remote(mine, mine, r_send.at[7 + spot], r_recv.at[group], dev))
    arrived(pair_recv, p_recv.at[0])
    pair_hot[...] = (
        lax.broadcasted_iota(jnp.int32, (NDET, PAIRS), 0).astype(F32) == pair_recv[0:1]
    ).astype(F32).astype(BF16)
    for j in range(1, SLABS):
        other = lax.rem(group + j, SLABS)
        arrived(reads.at[other], r_recv.at[other])
    readings = jnp.sum(reads[...], axis=0)
    wide = jnp.concatenate([readings, jnp.zeros((6, NDET), F32)], axis=0)
    model = dot_parts(parts_of(wide), (pair_hot[...],), ((1,), (0,)))
    active = pair_recv[3:4]
    conj = jnp.concatenate(
        [
            (model[0:1] - pair_recv[1:2]) * active,
            (pair_recv[2:3] - model[1:2]) * active,
            jnp.zeros((6, PAIRS), F32),
        ],
        axis=0,
    )
    weights = dot_parts(parts_of(conj), (pair_hot[...],), ((1,), (1,)))
    for c in range(2):
        hot = lane_hot[...]
        pieces = [(hot * part.astype(F32)).astype(BF16) for part in parts_of(weights[c : c + 1])]
        right = dot_parts((place[...],), pieces, ((1,), (1,)))
        resid[c] = right
        direc_a[c, whole, :] = right * first
        field[1, c, whole, :] = right * first

    solve(1)

    @pl.loop(0, SLABS, unroll=4)
    def _(p):
        base = at(p + 1)
        refs = [[field.at[a, c] for c in range(2)] for a in range(2)]
        here = [[refs[a][c][pl.ds(base, SLOT), :] for c in range(2)] for a in range(2)]
        sides = (
            x_plus,
            x_minus,
            lambda ref, b: y_plus(ref, b, ref[pl.ds(b, SLOT), :]) * yp_in,
            lambda ref, b: y_minus(ref, b, ref[pl.ds(b, SLOT), :]) * ym_in,
            lambda ref, b: ref[pl.ds(b + SLOT, SLOT), :],
            lambda ref, b: ref[pl.ds(b - SLOT, SLOT), :],
        )
        total = jnp.zeros((SLOT, LANES), F32)
        for side in sides:
            gap = [[here[a][c] - side(refs[a][c], base) for c in range(2)] for a in range(2)]
            total = total + gap[0][0] * gap[1][0] - gap[0][1] * gap[1][1]
        grads[p, 0] = here[0][1] * here[1][1] - here[0][0] * here[1][0]
        grads[p, 1] = -0.5 * total
        for out in range(2):
            low, high = grads[p, out, pl.ds(7, 16), :], grads[p, out, pl.ds(8, 16), :]
            ysend[p, out] = pltpu.roll(jnp.where(lane[0:16] >= 64, low, high), 64, 1)

    across = [
        remote(ysend.at[pl.ds((dev[0] // 8) * 4, 4)], yrecv.at[j], y_send.at[j], y_recv.at[j], dev)
        for j, dev in enumerate(y_peers)
    ]
    for copy in across:
        copy.wait()
    for t in range(4):
        for out in range(2):
            total = ysend[my_y * 4 + t, out] + yrecv[0, t, out] + yrecv[1, t, out] + yrecv[2, t, out]
            fsend[t, 0, out] = total[0:8]
            grads[t, out, pl.ds(0, 16), :] = total
            low, high = grads[t, out, pl.ds(6, 8), :], grads[t, out, pl.ds(7, 8), :]
            fsend[t, 1, out] = pltpu.roll(jnp.where(lane[0:8] >= 32, low, high), 96, 1)

    def final_copy(t, h):
        return pltpu.make_async_remote_copy(
            src_ref=fsend.at[t, h],
            dst_ref=frecv.at[my_z // 2],
            send_sem=f_send.at[2 * t + h],
            recv_sem=f_recv.at[my_z // 2],
            device_id=final_to[t][h],
            device_id_type=MESH,
        )

    for t in range(4):
        for h in range(2):
            mine = is_me(final_to[t][h])

            @pl.when(jnp.logical_not(mine))
            def _():
                final_copy(t, h).start()

            @pl.when(mine)
            def _():
                pltpu.make_async_copy(fsend.at[t, h], frecv.at[my_z // 2], f_recv.at[my_z // 2]).start()

    for m in range(8):
        pltpu.make_async_copy(frecv.at[m], frecv.at[m], f_recv.at[m]).wait()
    for out, out_ref in enumerate((out_abs_ref, out_dif_ref)):
        total = frecv[0, out]
        for m in range(1, 8):
            total = total + frecv[m, out]
        for k in range(6):
            out_ref[0:1, pl.ds(128 * k, 128)] = total[k : k + 1]
        out_ref[0:1, pl.ds(768, 32)] = total[6:7, 0:32]
    for t in range(4):
        for h in range(2):

            @pl.when(jnp.logical_not(is_me(final_to[t][h])))
            def _():
                final_copy(t, h).wait_send()

    for copy in sent:
        copy.wait_send()


def body(source_field, kappa, absorb, det_cell, pair_det, pair_count, measured):
    tall = 216
    vmem = pl.BlockSpec(memory_space=pltpu.VMEM)
    stacked = (SLABS + 2) * SLOT
    flat = SLABS * SLOT
    out = jax.ShapeDtypeStruct((1, 800), F32)
    dma = pltpu.SemaphoreType.DMA
    return pl.pallas_call(
        kernel,
        out_shape=(out, out),
        in_specs=[pl.BlockSpec(memory_space=pltpu.SMEM)] + [vmem] * 6,
        out_specs=(vmem, vmem),
        scratch_shapes=[
            pltpu.VMEM((3, tall, LANES), F32),
            pltpu.VMEM((3, tall, LANES), F32),
            pltpu.VMEM((SLABS, 3, SLOT, LANES), F32),
            pltpu.VMEM((2, SLABS, SLOT, LANES), F32),
            pltpu.VMEM((SLABS, SLOT, LANES), F32),
            pltpu.VMEM((stacked, LANES), F32),
            pltpu.VMEM((7, flat, LANES), F32),
            pltpu.VMEM((2, stacked, LANES), F32),
            pltpu.VMEM((2, stacked, LANES), F32),
            pltpu.VMEM((2, flat, LANES), F32),
            pltpu.VMEM((2, 2, stacked, LANES), F32),
            pltpu.VMEM((SLABS, 2, SLOT, LANES), F32),
            pltpu.VMEM((flat, NDET), BF16),
            pltpu.VMEM((LANES, NDET), F32),
            pltpu.VMEM((NDET, PAIRS), BF16),
            pltpu.VMEM((8, PAIRS), F32),
            pltpu.VMEM((8, PAIRS), F32),
            pltpu.VMEM((SLABS, 2, NDET), F32),
            pltpu.VMEM((SLABS, 2, 16, LANES), F32),
            pltpu.VMEM((3, 4, 2, 16, LANES), F32),
            pltpu.VMEM((4, 2, 2, 8, LANES), F32),
            pltpu.VMEM((8, 2, 8, LANES), F32),
            dma((16,)), dma((16,)), dma((7,)), dma((7,)), dma((8,)), dma((8,)),
            dma((3,)), dma((3,)), dma((1,)), dma((1,)),
            dma((15,)), dma((16,)), dma((3,)), dma((3,)), dma((8,)), dma((8,)),
        ],
        compiler_params=pltpu.CompilerParams(
            collective_id=0, has_side_effects=True, vmem_limit_bytes=40 * 1024 * 1024
        ),
    )(
        pair_count,
        source_field.reshape(200, LANES),
        kappa.reshape(200, LANES),
        absorb.reshape(200, LANES),
        det_cell.reshape(1, NDET),
        pair_det,
        measured,
    )


def solution(mesh):
    placed = (
        P("src", "slab", None),
        P("slab", None),
        P("slab", None),
        P(),
        P("src", None),
        P("src"),
        P(None, "src", None),
    )
    return jax.shard_map(
        body,
        mesh=mesh,
        in_specs=placed,
        out_specs=(P("slab", "src"), P("slab", "src")),
        check_vma=False,
    )
```

time: 126 us -> 78.6 us (0.62)
  Pallas kernels: 119 us -> 72.6 us
    pallas_call x1, Pallas kernels: 119 us -> 72.6 us  [body(): pl.pallas_call(kernel, out_shape=(out, out), in_specs=[pl.BlockSpec(memor...]
where the time goes in v2:
time: 78.6 us; the launch traced here: 78.4 us
  Pallas kernels  72.6 us (92%)
  local copies, waits for them, and re-layouts  4.53 us (6%)
  between operations  1.31 us (2%)
    pallas_call x1, Pallas kernels, body(): pl.pallas_call(kernel, out_shape=(out, out), in_specs=[pl.BlockSpec(memor...  72.6 us
    unnamed x14, local copies, waits for them, and re-layouts  4.53 us

profile of v2, /device:TPU:1, one launch (start us, length us, event | category | flops | bytes accessed | tf_op | source)
XLA Modules:
  0.0 78.4 jit_solution(17634893225878358285)
XLA Ops:
  1.3 0.0 copy-start.4
  1.3 0.0 copy-start.3
  1.3 0.0 copy-start.5
  1.3 0.7 copy-done.4
  2.0 0.0 copy-done.3
  2.0 0.0 copy-done.5
  2.0 0.0 copy-start
  2.0 0.9 %copy-done = f32[1,1,25600]{2,1,0:T(1,128)S(1)} copy-done((f32[1,1,25600]{2,1,0:T(1,128)S(1)}, f32[1,1,25600]{2,1,0:T(1,128)}, u32[]{:S(2)}) %copy-start) | copy-done | bytes 102424
  2.9 0.0 copy-start.1
  2.9 0.9 %copy-done.1 = f32[1,25600]{1,0:T(1,128)S(1)} copy-done((f32[1,25600]{1,0:T(1,128)S(1)}, f32[1,25600]{1,0:T(1,128)}, u32[]{:S(2)}) %copy-start.1) | copy-done | bytes 102424
  3.8 0.0 copy-start.2
  3.8 0.9 %copy-done.2 = f32[1,25600]{1,0:T(1,128)S(1)} copy-done((f32[1,25600]{1,0:T(1,128)S(1)}, f32[1,25600]{1,0:T(1,128)}, u32[]{:S(2)}) %copy-start.2) | copy-done | bytes 102424
  4.7 72.6 %shard_map.86 = (f32[1,800]{1,0:T(1,128)S(1)}, f32[1,800]{1,0:T(1,128)S(1)}) custom-call(s32[1]{0:T(128)S(6)} %copy.11.count_ref, f32[200,128]{1,0:T(8,128)S(1)} %bitcast.4, f32[200,128]{1,0:T(8,128)S(1)} %bitcast.5, f32[200,128]{1,0:T(8,128)S(1)} %bitcast.6, s32[1,512]{1,0:T(1,128)S(1)} %bitcast.7, s32[1,256]{1,0:T(1,128)S(1)} %copy-done.5, ...), custom_call_target="tpu_custom_call" | custom-call | tf_op jit(solution)/shard_map/pallas_call | solution.py:430
  77.2 0.6 copy.12
  77.8 0.6 copy.13
Async XLA Ops:
  1.3 0.7 copy-start.4
  1.3 0.7 copy-start.3
  1.3 0.7 copy-start.5
  2.0 0.9 %copy-start = (f32[1,1,25600]{2,1,0:T(1,128)S(1)}, f32[1,1,25600]{2,1,0:T(1,128)}, u32[]{:S(2)}) copy-start(f32[1,1,25600]{2,1,0:T(1,128)} %param.7) | copy-start | bytes 307204
  2.9 0.9 %copy-start.1 = (f32[1,25600]{1,0:T(1,128)S(1)}, f32[1,25600]{1,0:T(1,128)}, u32[]{:S(2)}) copy-start(f32[1,25600]{1,0:T(1,128)} %param.8) | copy-start | bytes 307204
  3.8 0.9 %copy-start.2 = (f32[1,25600]{1,0:T(1,128)S(1)}, f32[1,25600]{1,0:T(1,128)}, u32[]{:S(2)}) copy-start(f32[1,25600]{1,0:T(1,128)} %param.9) | copy-start | bytes 307204

commit v3 on v2

v3 whole, which is shorter than its diff:
```python
import jax
import jax.numpy as jnp
from jax import lax
from jax.experimental import pallas as pl
from jax.experimental.pallas import tpu as pltpu
from jax.sharding import PartitionSpec as P

NY = 160
SWEEPS = 6
NDET = 512
PAIRS = 256
SLABS = 16
HALO = 6
OWN_ROWS = 20
OWN_PLANES = 8
PLANES = OWN_PLANES + HALO
SLOT = 40
LANES = 128
FLAT = PLANES * SLOT
STACKED = FLAT + 2 * SLOT
PLANE_ROWS = 200
TALL = 216
MESH = pl.DeviceIdType.MESH
F32 = jnp.float32
BF16 = jnp.bfloat16

spectrum_low = 0.02
spectrum_high = 25.0
frequency_shift = 0.3


def chebyshev_terms():
    theta = (spectrum_high + spectrum_low) / 2.0
    delta = (spectrum_high - spectrum_low) / 2.0
    sigma = theta / delta
    rho = 1.0 / sigma
    keeps = []
    pushes = []
    for sweep in range(SWEEPS - 1):
        rho_new = 1.0 / (2.0 * sigma - rho)
        keeps.append(rho_new * rho)
        pushes.append(2.0 * rho_new / delta)
        rho = rho_new
    return (1.0 / theta, keeps, pushes)


def parts_of(value):
    high = value.astype(BF16)
    rest = value - high.astype(F32)
    middle = rest.astype(BF16)
    low = (rest - middle.astype(F32)).astype(BF16)
    return (high, middle, low)


def dot_parts(lhs_parts, rhs_parts, dims):
    total = None
    for lhs in lhs_parts:
        for rhs in rhs_parts:
            term = lax.dot_general(lhs, rhs, (dims, ((), ())), preferred_element_type=F32)
            total = term if total is None else total + term
    return total


def slot_of(plane):
    return jnp.where(plane < OWN_PLANES, plane, SLABS - 1 - plane)


def kernel(
    count_ref, source_hbm, kappa_hbm, absorb_hbm, cell_hbm, pair_hbm, measured_hbm,
    out_abs_ref, out_dif_ref,
    planes, cell_ref, pair_ref, measured_ref,
    half_lane, send, coef_recv, source, kappa, coef, direc_a, direc_b, resid, field, grads,
    place, lane_hot, pair_hot, pair_send, pair_recv, reads, ysend, yrecv, fsend, frecv,
    i_sem, s_send, s_recv, k_send, k_recv, o_send, o_recv, g_send, g_recv, p_send, p_recv,
    t_send, t_recv, u_send, u_recv, r_send, r_recv, y_send, y_recv, f_send, f_recv,
):
    src = lax.axis_index("src")
    slab = lax.axis_index("slab")
    my_y = src // 8
    my_z = (slab // 8) * 8 + src % 8
    my_x = (slab % 8) // 2
    core = slab % 2
    upper = my_z // 8
    parity = my_z % 2
    pair_z = my_z - parity
    group = parity * 4 + my_x
    member = group * 2 + core
    solved = jnp.where((pair_z >= 4) & (pair_z <= 10), pair_z - 4, lax.rem(pair_z + 5, 16))
    own_zlo = src % 8
    goal_z = jnp.where(own_zlo % 2 == 0, own_zlo + 4, lax.rem(own_zlo + 11, 16))
    swap_z = jnp.where(own_zlo < 4, lax.rem(my_z + 12, 16), lax.rem(my_z + 4, 16))
    native = core == upper

    def device(y, z, x, c):
        return (y * 8 + lax.rem(z, 8), (z // 8) * 8 + x * 2 + c)

    def is_me(dev):
        return (dev[0] == src) & (dev[1] == slab)

    source_to = [device(my_y, goal_z + g // 4, g % 4, upper) for g in range(8)]
    source_from = [(my_y * 8 + solved, core * 8 + i) for i in range(8)]
    near = [device(my_y, my_z, lax.rem(slab % 8 + j, 8) // 2, lax.rem(slab % 8 + j, 8) % 2) for j in range(1, 8)]
    twin = [device(my_y, pair_z + 1 - parity, i // 2, i % 2) for i in range(8)]
    native_to = [device(my_y, my_z, x, upper) for x in range(4)]
    beyond_to = device(my_y, swap_z, lax.rem(my_x + 4 - my_y, 4), upper)
    beyond_from = [device(my_y, swap_z, lax.rem(my_x + my_y, 4), c) for c in range(2)]
    y_peers = [(lax.rem(my_y + j, 4) * 8 + own_zlo, slab) for j in range(1, 4)]
    other_core = (src, slab + 1 - 2 * core)

    def plane_of(slot, half):
        return jnp.where(half == 0, slot, SLABS - 1 - slot)

    final_to = [[(4 * group + h, plane_of(2 * my_y + t, core)) for h in range(4)] for t in range(2)]
    final_from = [
        device(slot_of(slab) // 2, 2 * m + src // 16, (src // 4) % 4, slab // 8) for m in range(8)
    ]

    barrier = pltpu.get_barrier_semaphore()
    to_self = jnp.int32(0)
    for dev in final_from:
        to_self = to_self + jnp.where(is_me(dev), 1, 0)

        @pl.when(jnp.logical_not(is_me(dev)))
        def _():
            pl.semaphore_signal(barrier, inc=1, device_id=dev, device_id_type=MESH)

    for dev in source_from + twin + y_peers + near:
        pl.semaphore_signal(barrier, inc=1, device_id=dev, device_id_type=MESH)

    @pl.when(jnp.logical_not(native))
    def _():
        for dev in beyond_from:
            pl.semaphore_signal(barrier, inc=1, device_id=dev, device_id_type=MESH)

    loads = [
        pltpu.make_async_copy(ref, dst, i_sem.at[n])
        for n, (ref, dst) in enumerate((
            (kappa_hbm, planes.at[0]), (absorb_hbm, planes.at[1]), (source_hbm, planes.at[2]),
            (cell_hbm, cell_ref), (pair_hbm, pair_ref), (measured_hbm, measured_ref),
        ))
    ]
    for load in loads:
        load.start()

    lane = lax.broadcasted_iota(jnp.int32, (SLOT, LANES), 1)
    flat = lax.broadcasted_iota(jnp.int32, (SLOT, LANES), 0) * LANES + lane
    row = ((flat >> 5) * 205) >> 10
    col = flat - row * NY
    first_row = OWN_ROWS * group - HALO
    real_row = row + first_row
    row_in = (real_row >= 0) & (real_row < 160)
    xp_in = (row_in & (real_row < 159)).astype(F32)
    xm_in = (row_in & (real_row > 0)).astype(F32)
    yp_in = (col < NY - 1).astype(F32)
    ym_in = (col > 0).astype(F32)

    def x_plus(ref, base):
        near_row, far_row = ref[pl.ds(base + 1, SLOT), :], ref[pl.ds(base + 2, SLOT), :]
        return pltpu.roll(jnp.where(lane >= 32, near_row, far_row), 96, 1)

    def x_minus(ref, base):
        near_row, far_row = ref[pl.ds(base - 1, SLOT), :], ref[pl.ds(base - 2, SLOT), :]
        return pltpu.roll(jnp.where(lane < 96, near_row, far_row), 32, 1)

    def y_plus(ref, base, here):
        return pltpu.roll(jnp.where(lane >= 1, here, ref[pl.ds(base + 1, SLOT), :]), 127, 1)

    def y_minus(ref, base, here):
        return pltpu.roll(jnp.where(lane < 127, here, ref[pl.ds(base - 1, SLOT), :]), 1, 1)

    def at(p):
        return pl.multiple_of(p * SLOT, 8)

    for load in loads:
        load.wait()
    for which in range(3):
        half_lane[which, pl.ds(0, 8), :] = jnp.zeros((8, LANES), F32)
        half_lane[which, pl.ds(8, PLANE_ROWS), :] = pltpu.roll(planes[which], 64, 1)
        half_lane[which, pl.ds(8 + PLANE_ROWS, 8), :] = jnp.zeros((8, LANES), F32)
        for g in range(8):
            send[g, which] = jnp.where(
                lane < 64, half_lane[which, pl.ds(25 * g, SLOT), :], half_lane[which, pl.ds(25 * g + 1, SLOT), :]
            )
    active = (lax.broadcasted_iota(jnp.int32, (1, PAIRS), 1) < count_ref[0]).astype(F32)
    pair_send[...] = jnp.concatenate(
        [pair_ref[...].astype(F32), measured_ref[0], measured_ref[1], active, jnp.zeros((4, PAIRS), F32)],
        axis=0,
    )

    def remote_copy(src_ref, dst_ref, send_sem, recv_sem, dev):
        return pltpu.make_async_remote_copy(
            src_ref=src_ref, dst_ref=dst_ref, send_sem=send_sem, recv_sem=recv_sem,
            device_id=dev, device_id_type=MESH,
        )

    def remote(*args):
        copy = remote_copy(*args)
        copy.start()
        return copy

    def arrived(ref, sem):
        pltpu.make_async_copy(ref, ref, sem).wait()

    two = pl.ds(0, 2)
    my_slot = slot_of(slab)
    pl.semaphore_wait(barrier, 8 + 8 + 3 + 7 + 1 + 8 - to_self)
    sent = [remote(
        send.at[parity * 4 + lax.rem(my_x + 4 - my_y, 4), two], coef_recv.at[:, my_slot],
        o_send.at[0], o_recv.at[core], beyond_to,
    )]
    for g, dev in enumerate(source_to):
        sent.append(remote(send.at[g, 2], source.at[my_slot], s_send.at[g], s_recv.at[my_slot], dev))

    def native_copy(x):
        return remote_copy(
            send.at[parity * 4 + x, two], coef_recv.at[:, my_slot], k_send.at[x], k_recv.at[my_slot], native_to[x]
        )

    for x in range(4):

        @pl.when(jnp.logical_not(is_me(native_to[x])))
        def _():
            native_copy(x).start()

    sent.append(remote(
        pair_send, pair_recv, p_send.at[0], p_recv.at[0],
        device(my_y, goal_z + (slab % 8) // 4, slab % 4, upper),
    ))

    guard = jnp.zeros((SLOT, LANES), F32)
    last = (PLANES + 1) * SLOT
    for start in (0, last):
        kappa[pl.ds(start, SLOT), :] = guard
        for c in range(2):
            direc_a[c, pl.ds(start, SLOT), :] = guard
            direc_b[c, pl.ds(start, SLOT), :] = guard
            for a in range(2):
                field[a, c, pl.ds(start, SLOT), :] = guard

    cell = cell_ref[...]
    det_z = ((cell >> 10) * 1311) >> 15
    in_plane = cell - det_z * 25600
    det_x = ((in_plane >> 5) * 6554) >> 15
    det_y = in_plane - det_x * NY
    det_row = det_x - first_row
    det_slot = plane_of(det_z, core)
    in_window = (det_row >= 0) & (det_row < OWN_ROWS + 2 * HALO) & (det_slot < PLANES)
    owned = (
        (det_row >= HALO) & (det_row < HALO + OWN_ROWS) & (det_slot < OWN_PLANES)
    ).astype(F32)
    spot = det_row * NY + det_y
    det_sub = jnp.where(in_window, det_slot * SLOT + (spot >> 7), -1)
    det_lane = spot & 127

    @pl.loop(0, FLAT // 16, unroll=5)
    def _(p):
        subs = lax.broadcasted_iota(jnp.int32, (16, NDET), 0) + p * 16
        place[pl.ds(pl.multiple_of(p * 16, 16), 16), :] = (subs == det_sub).astype(F32).astype(BF16)

    lane_hot[...] = (lax.broadcasted_iota(jnp.int32, (LANES, NDET), 0) == det_lane).astype(F32)

    def pass_on(slot, both):
        n = slot - 2
        if both:
            return remote_copy(
                coef_recv.at[:, slot], coef_recv.at[:, SLABS - 1 - slot], t_send.at[n], t_recv.at[n], other_core
            )
        return remote_copy(
            source.at[slot], source.at[SLABS - 1 - slot], u_send.at[n], u_recv.at[n], other_core
        )

    @pl.when(native)
    def _():
        coef_recv[:, my_slot] = send[group, 0:2]
        for j in range(1, 8):
            slot = lax.rem(my_slot + j, 8)
            arrived(coef_recv.at[:, slot], k_recv.at[slot])

    @pl.when(jnp.logical_not(native))
    def _():
        far_x = lax.rem(my_x + my_y, 4)
        low = jnp.where(core == 0, 2 * far_x, 6 - 2 * far_x)
        for c in range(2):
            slot = jnp.where(core == 0, 2 * far_x + c, 7 - 2 * far_x - c)
            arrived(coef_recv.at[:, slot], o_recv.at[c])
        strips = coef_recv.at[:, pl.ds(low, 2)]
        across = [remote(strips, strips, g_send.at[j], g_recv.at[j], dev) for j, dev in enumerate(y_peers)]
        for copy in across:
            copy.wait()

    for slot in range(2, 8):
        sent.append(pass_on(slot, True))
        sent[-1].start()
    for n in range(6):
        arrived(coef_recv.at[:, OWN_PLANES + 5 - n], t_recv.at[n])

    @pl.loop(0, PLANES, unroll=7)
    def _(p):
        kappa[pl.ds(at(p + 1), SLOT), :] = coef_recv[0, p]

    @pl.loop(0, PLANES, unroll=7)
    def _(p):
        base, here = at(p + 1), at(p)
        k = kappa[pl.ds(base, SLOT), :]
        diagonal = coef_recv[1, p]
        beside = (
            (x_plus(kappa, base), xp_in),
            (x_minus(kappa, base), xm_in),
            (y_plus(kappa, base, k) * yp_in, yp_in),
            (y_minus(kappa, base, k) * ym_in, ym_in),
            (kappa[pl.ds(base + SLOT, SLOT), :], jnp.where(p < PLANES - 1, 1.0, 0.0).astype(F32)),
            (kappa[pl.ds(base - SLOT, SLOT), :], jnp.where(p > 0, 1.0, 0.0).astype(F32)),
        )
        for which, (side, inside) in enumerate(beside):
            face = (k + side) * 0.5
            diagonal = diagonal + face
            coef[which, pl.ds(here, SLOT), :] = face * inside
        coef[6, pl.ds(here, SLOT), :] = diagonal

    for slot in range(8):
        arrived(source.at[slot], s_recv.at[slot])
        if slot >= 2:
            sent.append(pass_on(slot, False))
            sent[-1].start()
    for n in range(6):
        arrived(source.at[OWN_PLANES + 5 - n], u_recv.at[n])

    first, keeps, pushes = chebyshev_terms()

    @pl.loop(0, PLANES, unroll=7)
    def _(p):
        base, here = at(p + 1), at(p)
        b = source[p]
        nothing = jnp.zeros_like(b)
        resid[0, pl.ds(here, SLOT), :] = b
        resid[1, pl.ds(here, SLOT), :] = nothing
        direc_a[0, pl.ds(base, SLOT), :] = b * first
        direc_a[1, pl.ds(base, SLOT), :] = nothing
        field[0, 0, pl.ds(base, SLOT), :] = b * first
        field[0, 1, pl.ds(base, SLOT), :] = nothing

    def solve(out):
        for sweep in range(SWEEPS - 1):
            keep, push = keeps[sweep], pushes[sweep]
            now, later = (direc_a, direc_b) if sweep % 2 == 0 else (direc_b, direc_a)
            count = PLANES - 1 - sweep

            def one_plane(p, kept):
                here, base = at(p), at(p + 1)
                cs = [coef[which, pl.ds(here, SLOT), :] for which in range(7)]
                ds = [now[c, pl.ds(base, SLOT), :] for c in range(2)]
                turned = (-ds[1], ds[0])
                for c in range(2):

                    def shifted(amount):
                        return now[c, pl.ds(base + amount, SLOT), :]

                    up, down = shifted(1), shifted(-1)
                    off = (
                        cs[0] * pltpu.roll(jnp.where(lane >= 32, up, shifted(2)), 96, 1)
                        + cs[1] * pltpu.roll(jnp.where(lane < 96, down, shifted(-2)), 32, 1)
                        + cs[2] * pltpu.roll(jnp.where(lane >= 1, ds[c], up), 127, 1)
                        + cs[3] * pltpu.roll(jnp.where(lane < 127, ds[c], down), 1, 1)
                        + cs[4] * shifted(SLOT)
                        + cs[5] * shifted(-SLOT)
                    )
                    applied = cs[6] * ds[c] - off + frequency_shift * turned[c]
                    left = resid[c, pl.ds(here, SLOT), :] - applied
                    resid[c, pl.ds(here, SLOT), :] = left
                    new = keep * ds[c] + push * left
                    later[c, pl.ds(base, SLOT), :] = new
                    if kept:
                        field[out, c, pl.ds(base, SLOT), :] = field[out, c, pl.ds(base, SLOT), :] + new

            @pl.loop(0, OWN_PLANES + 1, unroll=OWN_PLANES + 1)
            def _(p):
                one_plane(p, True)

            if count > OWN_PLANES + 1:

                @pl.loop(OWN_PLANES + 1, count, unroll=count - OWN_PLANES - 1)
                def _(p):
                    one_plane(p, False)

    solve(0)

    whole = pl.ds(SLOT, FLAT)
    mine_rows = OWN_PLANES * SLOT
    for c in range(2):
        spread = dot_parts(
            parts_of(field[0, c, pl.ds(SLOT, mine_rows), :]), (place[pl.ds(0, mine_rows), :],), ((0,), (0,))
        )
        reads[member, pl.ds(c, 1), :] = jnp.sum(spread * lane_hot[...], axis=0, keepdims=True) * owned
    mine = reads.at[member]
    for i, dev in enumerate(twin + near):
        sent.append(remote(mine, mine, r_send.at[i], r_recv.at[member], dev))
    arrived(pair_recv, p_recv.at[0])
    pair_hot[...] = (
        lax.broadcasted_iota(jnp.int32, (NDET, PAIRS), 0).astype(F32) == pair_recv[0:1]
    ).astype(F32).astype(BF16)
    for j in range(1, SLABS):
        other = lax.rem(member + j, SLABS)
        arrived(reads.at[other], r_recv.at[other])
    readings = jnp.sum(reads[...], axis=0)
    wide = jnp.concatenate([readings, jnp.zeros((6, NDET), F32)], axis=0)
    model = dot_parts(parts_of(wide), (pair_hot[...],), ((1,), (0,)))
    active = pair_recv[3:4]
    conj = jnp.concatenate(
        [
            (model[0:1] - pair_recv[1:2]) * active,
            (pair_recv[2:3] - model[1:2]) * active,
            jnp.zeros((6, PAIRS), F32),
        ],
        axis=0,
    )
    weights = dot_parts(parts_of(conj), (pair_hot[...],), ((1,), (1,)))
    for c in range(2):
        hot = lane_hot[...]
        pieces = [(hot * part.astype(F32)).astype(BF16) for part in parts_of(weights[c : c + 1])]
        right = dot_parts((place[...],), pieces, ((1,), (1,)))
        resid[c] = right
        direc_a[c, whole, :] = right * first
        field[1, c, whole, :] = right * first

    solve(1)

    @pl.loop(0, OWN_PLANES, unroll=4)
    def _(p):
        base = at(p + 1)
        refs = [[field.at[a, c] for c in range(2)] for a in range(2)]
        here = [[refs[a][c][pl.ds(base, SLOT), :] for c in range(2)] for a in range(2)]
        sides = (
            x_plus,
            x_minus,
            lambda ref, b: y_plus(ref, b, ref[pl.ds(b, SLOT), :]) * yp_in,
            lambda ref, b: y_minus(ref, b, ref[pl.ds(b, SLOT), :]) * ym_in,
            lambda ref, b: ref[pl.ds(b + SLOT, SLOT), :],
            lambda ref, b: ref[pl.ds(b - SLOT, SLOT), :],
        )
        total = jnp.zeros((SLOT, LANES), F32)
        for side in sides:
            gap = [[here[a][c] - side(refs[a][c], base) for c in range(2)] for a in range(2)]
            total = total + gap[0][0] * gap[1][0] - gap[0][1] * gap[1][1]
        grads[p, 0] = here[0][1] * here[1][1] - here[0][0] * here[1][0]
        grads[p, 1] = -0.5 * total
        for out in range(2):
            low, high = grads[p, out, pl.ds(7, 32), :], grads[p, out, pl.ds(8, 32), :]
            ysend[p, out] = pltpu.roll(jnp.where(lane[0:32] >= 64, low, high), 64, 1)

    across = [
        remote(ysend.at[pl.ds((dev[0] // 8) * 2, 2)], yrecv.at[j], y_send.at[j], y_recv.at[j], dev)
        for j, dev in enumerate(y_peers)
    ]
    for copy in across:
        copy.wait()
    for t in range(2):
        for out in range(2):
            grads[t, out, pl.ds(0, 32), :] = (
                ysend[my_y * 2 + t, out] + yrecv[0, t, out] + yrecv[1, t, out] + yrecv[2, t, out]
            )
            for h in range(4):
                start = (25 * h) // 4
                low, high = grads[t, out, pl.ds(start, 8), :], grads[t, out, pl.ds(start + 1, 8), :]
                if h == 0:
                    fsend[t, h, out] = low
                else:
                    fsend[t, h, out] = pltpu.roll(jnp.where(lane[0:8] >= 32 * h, low, high), 128 - 32 * h, 1)

    def final_copy(t, h):
        return remote_copy(
            fsend.at[t, h], frecv.at[my_z // 2], f_send.at[4 * t + h], f_recv.at[my_z // 2], final_to[t][h]
        )

    for t in range(2):
        for h in range(4):
            own = is_me(final_to[t][h])

            @pl.when(jnp.logical_not(own))
            def _():
                final_copy(t, h).start()

            @pl.when(own)
            def _():
                pltpu.make_async_copy(fsend.at[t, h], frecv.at[my_z // 2], f_recv.at[my_z // 2]).start()

    for x in range(4):

        @pl.when(jnp.logical_not(is_me(native_to[x])))
        def _():
            native_copy(x).wait_send()

    for copy in sent:
        copy.wait_send()
    for m in range(8):
        arrived(frecv.at[m], f_recv.at[m])
    for out, out_ref in enumerate((out_abs_ref, out_dif_ref)):
        total = frecv[0, out]
        for m in range(1, 8):
            total = total + frecv[m, out]
        for k in range(6):
            out_ref[0:1, pl.ds(128 * k, 128)] = total[k : k + 1]
        out_ref[0:1, pl.ds(768, 32)] = total[6:7, 0:32]
    for t in range(2):
        for h in range(4):

            @pl.when(jnp.logical_not(is_me(final_to[t][h])))
            def _():
                final_copy(t, h).wait_send()


def body(source_field, kappa, absorb, det_cell, pair_det, pair_count, measured):
    vmem = pl.BlockSpec(memory_space=pltpu.VMEM)
    hbm = pl.BlockSpec(memory_space=pltpu.HBM)
    out = jax.ShapeDtypeStruct((1, 800), F32)
    dma = pltpu.SemaphoreType.DMA
    return pl.pallas_call(
        kernel,
        out_shape=(out, out),
        in_specs=[pl.BlockSpec(memory_space=pltpu.SMEM)] + [hbm] * 6,
        out_specs=(vmem, vmem),
        scratch_shapes=[
            pltpu.VMEM((3, PLANE_ROWS, LANES), F32),
            pltpu.VMEM((1, NDET), jnp.int32),
            pltpu.VMEM((1, PAIRS), jnp.int32),
            pltpu.VMEM((2, 1, PAIRS), F32),
            pltpu.VMEM((3, TALL, LANES), F32),
            pltpu.VMEM((8, 3, SLOT, LANES), F32),
            pltpu.VMEM((2, PLANES, SLOT, LANES), F32),
            pltpu.VMEM((PLANES, SLOT, LANES), F32),
            pltpu.VMEM((STACKED, LANES), F32),
            pltpu.VMEM((7, FLAT, LANES), F32),
            pltpu.VMEM((2, STACKED, LANES), F32),
            pltpu.VMEM((2, STACKED, LANES), F32),
            pltpu.VMEM((2, FLAT, LANES), F32),
            pltpu.VMEM((2, 2, STACKED, LANES), F32),
            pltpu.VMEM((OWN_PLANES, 2, SLOT, LANES), F32),
            pltpu.VMEM((FLAT, NDET), BF16),
            pltpu.VMEM((LANES, NDET), F32),
            pltpu.VMEM((NDET, PAIRS), BF16),
            pltpu.VMEM((8, PAIRS), F32),
            pltpu.VMEM((8, PAIRS), F32),
            pltpu.VMEM((SLABS, 2, NDET), F32),
            pltpu.VMEM((OWN_PLANES, 2, 32, LANES), F32),
            pltpu.VMEM((3, 2, 2, 32, LANES), F32),
            pltpu.VMEM((2, 4, 2, 8, LANES), F32),
            pltpu.VMEM((8, 2, 8, LANES), F32),
            dma((6,)), dma((8,)), dma((8,)), dma((4,)), dma((8,)), dma((1,)), dma((2,)),
            dma((3,)), dma((3,)), dma((1,)), dma((1,)),
            dma((6,)), dma((6,)), dma((6,)), dma((6,)),
            dma((15,)), dma((16,)), dma((3,)), dma((3,)), dma((8,)), dma((8,)),
        ],
        compiler_params=pltpu.CompilerParams(
            collective_id=0, has_side_effects=True, vmem_limit_bytes=60 * 1024 * 1024
        ),
    )(
        pair_count,
        source_field.reshape(PLANE_ROWS, LANES),
        kappa.reshape(PLANE_ROWS, LANES),
        absorb.reshape(PLANE_ROWS, LANES),
        det_cell.reshape(1, NDET),
        pair_det,
        measured,
    )


def solution(mesh):
    placed = (
        P("src", "slab", None),
        P("slab", None),
        P("slab", None),
        P(),
        P("src", None),
        P("src"),
        P(None, "src", None),
    )
    return jax.shard_map(
        body,
        mesh=mesh,
        in_specs=placed,
        out_specs=(P("slab", "src"), P("slab", "src")),
        check_vma=False,
    )
```

time: 78.6 us -> 68.7 us (0.87)
  the two profiles are of different devices: /device:TPU:1 before, /device:TPU:5 now
where the time goes in v3:
time: 68.7 us; the launch traced here: 68.5 us
  Pallas kernels  65.3 us (95%)
  local copies, waits for them, and re-layouts  1.92 us (3%)
  between operations  1.3 us (2%)
    pallas_call x1, Pallas kernels, body(): pl.pallas_call(kernel, out_shape=(out, out), in_specs=[pl.BlockSpec(memor...  65.3 us
    unnamed x6, local copies, waits for them, and re-layouts  1.92 us

profile of v3, /device:TPU:5, one launch (start us, length us, event | category | flops | bytes accessed | tf_op | source)
XLA Modules:
  0.0 68.5 jit_solution(18178185000276919364)
XLA Ops:
  1.3 65.3 %shard_map.86 = (f32[1,800]{1,0:T(1,128)}, f32[1,800]{1,0:T(1,128)}) custom-call(s32[1]{0:T(128)S(6)} %copy.11.count_ref, f32[200,128]{1,0:T(8,128)} %bitcast.4, f32[200,128]{1,0:T(8,128)} %bitcast.5, f32[200,128]{1,0:T(8,128)} %bitcast.6, s32[1,512]{1,0:T(1,128)} %bitcast.7, s32[1,256]{1,0:T(1,128)} %pair_hbm.1, f32[2,1,256]{2,1,0:T(1,128)} %measured_hbm.1), custom_call_target="tpu_custom_call" | custom-call | tf_op jit(solution)/shard_map/pallas_call | solution.py:516
  66.6 0.0 copy-start.1
  66.6 0.7 copy-done.1
  67.2 0.0 copy-start
  67.2 0.6 copy.12
  67.8 0.1 copy-done
  67.9 0.6 copy.13
Async XLA Ops:
  66.6 0.7 copy-start.1
  67.2 0.7 copy-start

commit v4 on v3

--- a/solution.py
+++ b/solution.py
@@ -66,11 +66,11 @@
 
 
 def kernel(
-    count_ref, source_hbm, kappa_hbm, absorb_hbm, cell_hbm, pair_hbm, measured_hbm,
-    out_abs_ref, out_dif_ref,
-    planes, cell_ref, pair_ref, measured_ref,
+    count_hbm, source_hbm, kappa_hbm, absorb_hbm, cell_hbm, pair_hbm, measured_hbm,
+    out_ref,
+    planes, count_ref, cell_ref, pair_ref, measured_ref,
     half_lane, send, coef_recv, source, kappa, coef, direc_a, direc_b, resid, field, grads,
-    place, lane_hot, pair_hot, pair_send, pair_recv, reads, ysend, yrecv, fsend, frecv,
+    place, lane_hot, pair_hot, pair_send, pair_recv, reads, ysend, yrecv, ysum, fsend, frecv,
     i_sem, s_send, s_recv, k_send, k_recv, o_send, o_recv, g_send, g_recv, p_send, p_recv,
     t_send, t_recv, u_send, u_recv, r_send, r_recv, y_send, y_recv, f_send, f_recv,
 ):
@@ -83,7 +83,7 @@
     upper = my_z // 8
     parity = my_z % 2
     pair_z = my_z - parity
-    group = parity * 4 + my_x
+    group = my_x * 2 + parity
     member = group * 2 + core
     solved = jnp.where((pair_z >= 4) & (pair_z <= 10), pair_z - 4, lax.rem(pair_z + 5, 16))
     own_zlo = src % 8
@@ -97,7 +97,7 @@
     def is_me(dev):
         return (dev[0] == src) & (dev[1] == slab)
 
-    source_to = [device(my_y, goal_z + g // 4, g % 4, upper) for g in range(8)]
+    source_to = [device(my_y, goal_z + g % 2, g // 2, upper) for g in range(8)]
     source_from = [(my_y * 8 + solved, core * 8 + i) for i in range(8)]
     near = [device(my_y, my_z, lax.rem(slab % 8 + j, 8) // 2, lax.rem(slab % 8 + j, 8) % 2) for j in range(1, 8)]
     twin = [device(my_y, pair_z + 1 - parity, i // 2, i % 2) for i in range(8)]
@@ -110,10 +110,13 @@
     def plane_of(slot, half):
         return jnp.where(half == 0, slot, SLABS - 1 - slot)
 
-    final_to = [[(4 * group + h, plane_of(2 * my_y + t, core)) for h in range(4)] for t in range(2)]
-    final_from = [
-        device(slot_of(slab) // 2, 2 * m + src // 16, (src // 4) % 4, slab // 8) for m in range(8)
-    ]
+    row_to = []
+    for q in range(OWN_PLANES):
+        p = plane_of(q, core) % 8
+        row_to.append(device(my_x, my_z, p // 2, p % 2))
+    row_from = [device(lax.rem(my_y + j, 4), my_z, my_y, c) for j in range(1, 4) for c in range(2)]
+    final_to = [[device(my_y, 8 * c + 4 * parity + h, my_x, core) for h in range(4)] for c in range(2)]
+    final_from = [device(my_y, 2 * m + own_zlo // 4, my_x, core) for m in range(8)]
 
     barrier = pltpu.get_barrier_semaphore()
     to_self = jnp.int32(0)
@@ -124,19 +127,19 @@
         def _():
             pl.semaphore_signal(barrier, inc=1, device_id=dev, device_id_type=MESH)
 
-    for dev in source_from + twin + y_peers + near:
+    for dev in source_from + twin + row_from + near:
         pl.semaphore_signal(barrier, inc=1, device_id=dev, device_id_type=MESH)
 
     @pl.when(jnp.logical_not(native))
     def _():
-        for dev in beyond_from:
+        for dev in beyond_from + y_peers:
             pl.semaphore_signal(barrier, inc=1, device_id=dev, device_id_type=MESH)
 
     loads = [
         pltpu.make_async_copy(ref, dst, i_sem.at[n])
         for n, (ref, dst) in enumerate((
             (kappa_hbm, planes.at[0]), (absorb_hbm, planes.at[1]), (source_hbm, planes.at[2]),
-            (cell_hbm, cell_ref), (pair_hbm, pair_ref), (measured_hbm, measured_ref),
+            (cell_hbm, cell_ref), (count_hbm, count_ref), (pair_hbm, pair_ref), (measured_hbm, measured_ref),
         ))
     ]
     for load in loads:
@@ -203,9 +206,10 @@
 
     two = pl.ds(0, 2)
     my_slot = slot_of(slab)
-    pl.semaphore_wait(barrier, 8 + 8 + 3 + 7 + 1 + 8 - to_self)
+    rows_leave = jnp.where(my_x == my_y, 0, 8)
+    pl.semaphore_wait(barrier, 8 + 8 + 7 + 1 + 8 - to_self + rows_leave + jnp.where(native, 0, 3))
     sent = [remote(
-        send.at[parity * 4 + lax.rem(my_x + 4 - my_y, 4), two], coef_recv.at[:, my_slot],
+        send.at[2 * lax.rem(my_x + 4 - my_y, 4) + parity, two], coef_recv.at[:, my_slot],
         o_send.at[0], o_recv.at[core], beyond_to,
     )]
     for g, dev in enumerate(source_to):
@@ -213,7 +217,7 @@
 
     def native_copy(x):
         return remote_copy(
-            send.at[parity * 4 + x, two], coef_recv.at[:, my_slot], k_send.at[x], k_recv.at[my_slot], native_to[x]
+            send.at[2 * x + parity, two], coef_recv.at[:, my_slot], k_send.at[x], k_recv.at[my_slot], native_to[x]
         )
 
     for x in range(4):
@@ -224,7 +228,7 @@
 
     sent.append(remote(
         pair_send, pair_recv, p_send.at[0], p_recv.at[0],
-        device(my_y, goal_z + (slab % 8) // 4, slab % 4, upper),
+        device(my_y, goal_z + slab % 2, (slab % 8) // 2, upper),
     ))
 
     guard = jnp.zeros((SLOT, LANES), F32)
@@ -424,9 +428,13 @@
 
     solve(1)
 
-    @pl.loop(0, OWN_PLANES, unroll=4)
-    def _(p):
-        base = at(p + 1)
+    def row_copy(q):
+        return remote_copy(
+            ysend.at[q], yrecv.at[core, my_y], y_send.at[q], y_recv.at[core, my_y], row_to[q]
+        )
+
+    for q in range(OWN_PLANES):
+        base = (q + 1) * SLOT
         refs = [[field.at[a, c] for c in range(2)] for a in range(2)]
         here = [[refs[a][c][pl.ds(base, SLOT), :] for c in range(2)] for a in range(2)]
         sides = (
@@ -441,85 +449,94 @@
         for side in sides:
             gap = [[here[a][c] - side(refs[a][c], base) for c in range(2)] for a in range(2)]
             total = total + gap[0][0] * gap[1][0] - gap[0][1] * gap[1][1]
-        grads[p, 0] = here[0][1] * here[1][1] - here[0][0] * here[1][0]
-        grads[p, 1] = -0.5 * total
+        grads[q, 0] = here[0][0] * here[1][0] - here[0][1] * here[1][1]
+        grads[q, 1] = total
         for out in range(2):
-            low, high = grads[p, out, pl.ds(7, 32), :], grads[p, out, pl.ds(8, 32), :]
-            ysend[p, out] = pltpu.roll(jnp.where(lane[0:32] >= 64, low, high), 64, 1)
-
-    across = [
-        remote(ysend.at[pl.ds((dev[0] // 8) * 2, 2)], yrecv.at[j], y_send.at[j], y_recv.at[j], dev)
-        for j, dev in enumerate(y_peers)
-    ]
-    for copy in across:
-        copy.wait()
-    for t in range(2):
-        for out in range(2):
-            grads[t, out, pl.ds(0, 32), :] = (
-                ysend[my_y * 2 + t, out] + yrecv[0, t, out] + yrecv[1, t, out] + yrecv[2, t, out]
-            )
-            for h in range(4):
-                start = (25 * h) // 4
-                low, high = grads[t, out, pl.ds(start, 8), :], grads[t, out, pl.ds(start + 1, 8), :]
+            low, high = grads[q, out, pl.ds(7, 32), :], grads[q, out, pl.ds(8, 32), :]
+            rows = pltpu.roll(jnp.where(lane[0:32] >= 64, low, high), 64, 1)
+            ysend[q, pl.ds(25 * out, 25), :] = rows[0:25]
+        ysend[q, pl.ds(50, 6), :] = jnp.zeros((6, LANES), F32)
+        stays = is_me(row_to[q])
+
+        @pl.when(jnp.logical_not(stays))
+        def _():
+            row_copy(q).start()
+
+        @pl.when(stays)
+        def _():
+            pltpu.make_async_copy(ysend.at[q], yrecv.at[core, my_y], y_recv.at[core, my_y]).start()
+
+    def final_copy(c, h):
+        return remote_copy(
+            fsend.at[c, h], frecv.at[my_z // 2], f_send.at[4 * c + h], f_recv.at[my_z // 2], final_to[c][h]
+        )
+
+    for c in range(2):
+        for y in range(4):
+            arrived(yrecv.at[c, y], y_recv.at[c, y])
+        ysum[c] = (yrecv[c, 0] + yrecv[c, 1]) + (yrecv[c, 2] + yrecv[c, 3])
+        for h in range(4):
+            for out in range(2):
+                start = 25 * out + (25 * h) // 4
+                low, high = ysum[c, pl.ds(start, 8), :], ysum[c, pl.ds(start + 1, 8), :]
                 if h == 0:
-                    fsend[t, h, out] = low
+                    fsend[c, h, out] = low
                 else:
-                    fsend[t, h, out] = pltpu.roll(jnp.where(lane[0:8] >= 32 * h, low, high), 128 - 32 * h, 1)
-
-    def final_copy(t, h):
-        return remote_copy(
-            fsend.at[t, h], frecv.at[my_z // 2], f_send.at[4 * t + h], f_recv.at[my_z // 2], final_to[t][h]
-        )
-
-    for t in range(2):
-        for h in range(4):
-            own = is_me(final_to[t][h])
+                    fsend[c, h, out] = pltpu.roll(jnp.where(lane[0:8] >= 32 * h, low, high), 128 - 32 * h, 1)
+            own = is_me(final_to[c][h])
 
             @pl.when(jnp.logical_not(own))
             def _():
-                final_copy(t, h).start()
+                final_copy(c, h).start()
 
             @pl.when(own)
             def _():
-                pltpu.make_async_copy(fsend.at[t, h], frecv.at[my_z // 2], f_recv.at[my_z // 2]).start()
+                pltpu.make_async_copy(fsend.at[c, h], frecv.at[my_z // 2], f_recv.at[my_z // 2]).start()
 
     for x in range(4):
 
         @pl.when(jnp.logical_not(is_me(native_to[x])))
         def _():
             native_copy(x).wait_send()
+
+    for q in range(OWN_PLANES):
+
+        @pl.when(jnp.logical_not(is_me(row_to[q])))
+        def _():
+            row_copy(q).wait_send()
 
     for copy in sent:
         copy.wait_send()
     for m in range(8):
         arrived(frecv.at[m], f_recv.at[m])
-    for out, out_ref in enumerate((out_abs_ref, out_dif_ref)):
+    for out in range(2):
         total = frecv[0, out]
         for m in range(1, 8):
             total = total + frecv[m, out]
         for k in range(6):
-            out_ref[0:1, pl.ds(128 * k, 128)] = total[k : k + 1]
-        out_ref[0:1, pl.ds(768, 32)] = total[6:7, 0:32]
-    for t in range(2):
+            out_ref[out, 0:1, pl.ds(128 * k, 128)] = total[k : k + 1]
+        out_ref[out, 0:1, pl.ds(768, 32)] = total[6:7, 0:32]
+    for c in range(2):
         for h in range(4):
 
-            @pl.when(jnp.logical_not(is_me(final_to[t][h])))
+            @pl.when(jnp.logical_not(is_me(final_to[c][h])))
             def _():
-                final_copy(t, h).wait_send()
+                final_copy(c, h).wait_send()
 
 
 def body(source_field, kappa, absorb, det_cell, pair_det, pair_count, measured):
     vmem = pl.BlockSpec(memory_space=pltpu.VMEM)
     hbm = pl.BlockSpec(memory_space=pltpu.HBM)
-    out = jax.ShapeDtypeStruct((1, 800), F32)
+    out = jax.ShapeDtypeStruct((2, 1, 800), F32)
     dma = pltpu.SemaphoreType.DMA
-    return pl.pallas_call(
+    sums = pl.pallas_call(
         kernel,
-        out_shape=(out, out),
-        in_specs=[pl.BlockSpec(memory_space=pltpu.SMEM)] + [hbm] * 6,
-        out_specs=(vmem, vmem),
+        out_shape=out,
+        in_specs=[hbm] * 7,
+        out_specs=vmem,
         scratch_shapes=[
             pltpu.VMEM((3, PLANE_ROWS, LANES), F32),
+            pltpu.SMEM((1,), jnp.int32),
             pltpu.VMEM((1, NDET), jnp.int32),
             pltpu.VMEM((1, PAIRS), jnp.int32),
             pltpu.VMEM((2, 1, PAIRS), F32),
@@ -540,14 +557,15 @@
             pltpu.VMEM((8, PAIRS), F32),
             pltpu.VMEM((8, PAIRS), F32),
             pltpu.VMEM((SLABS, 2, NDET), F32),
-            pltpu.VMEM((OWN_PLANES, 2, 32, LANES), F32),
-            pltpu.VMEM((3, 2, 2, 32, LANES), F32),
+            pltpu.VMEM((OWN_PLANES, 56, LANES), F32),
+            pltpu.VMEM((2, 4, 56, LANES), F32),
+            pltpu.VMEM((2, 56, LANES), F32),
             pltpu.VMEM((2, 4, 2, 8, LANES), F32),
             pltpu.VMEM((8, 2, 8, LANES), F32),
-            dma((6,)), dma((8,)), dma((8,)), dma((4,)), dma((8,)), dma((1,)), dma((2,)),
+            dma((7,)), dma((8,)), dma((8,)), dma((4,)), dma((8,)), dma((1,)), dma((2,)),
             dma((3,)), dma((3,)), dma((1,)), dma((1,)),
             dma((6,)), dma((6,)), dma((6,)), dma((6,)),
-            dma((15,)), dma((16,)), dma((3,)), dma((3,)), dma((8,)), dma((8,)),
+            dma((15,)), dma((16,)), dma((8,)), dma((2, 4)), dma((8,)), dma((8,)),
         ],
         compiler_params=pltpu.CompilerParams(
             collective_id=0, has_side_effects=True, vmem_limit_bytes=60 * 1024 * 1024
@@ -561,6 +579,7 @@
         pair_det,
         measured,
     )
+    return (-sums[0], -0.5 * sums[1])
 
 
 def solution(mesh):

time: 68.7 us -> 63.4 us (0.923)
  the two profiles are of different devices: /device:TPU:5 before, /device:TPU:25 now
where the time goes in v4:
time: 63.4 us; the launch traced here: 63.3 us
  Pallas kernels  60.7 us (96%)
  between operations  1.29 us (2%)
  other arithmetic  1.27 us (2%)
    pallas_call x1, Pallas kernels, body(): pl.pallas_call(kernel, out_shape=out, in_specs=[hbm] * 7, out_specs=vmem,...  60.7 us

profile of v4, /device:TPU:25, one launch (start us, length us, event | category | flops | bytes accessed | tf_op | source)
XLA Modules:
  0.0 63.3 jit_solution(11247688398327999902)
XLA Ops:
  1.3 60.7 %shard_map.86 = f32[2,1,800]{2,1,0:T(1,128)} custom-call(s32[1]{0:T(128)S(6)} %copy.9.count_hbm, f32[200,128]{1,0:T(8,128)} %bitcast.8, f32[200,128]{1,0:T(8,128)} %bitcast.9, f32[200,128]{1,0:T(8,128)} %bitcast.10, s32[1,512]{1,0:T(1,128)} %bitcast.11, s32[1,256]{1,0:T(1,128)} %pair_hbm.1, f32[2,1,256]{2,1,0:T(1,128)} %measured_hbm.1), custom_call_target="tpu_custom_call" | custom-call | tf_op jit(solution)/shard_map/pallas_call | solution.py:532
  62.0 1.3 %multiply_bitcast_fusion = (f32[1,800]{1,0:T(1,128)}, f32[1,800]{1,0:T(1,128)}) fusion(f32[2,1,800]{2,1,0:T(1,128)} %shard_map.86), kind=kLoop, calls=%fused_computation | loop fusion | flops 1600 | bytes 12800 | tf_op jit(solution)/shard_map/mul | solution.py:582

commit v5 on v4

--- a/solution.py
+++ b/solution.py
@@ -52,13 +52,14 @@
     return (high, middle, low)
 
 
-def dot_parts(lhs_parts, rhs_parts, dims):
-    total = None
-    for lhs in lhs_parts:
-        for rhs in rhs_parts:
-            term = lax.dot_general(lhs, rhs, (dims, ((), ())), preferred_element_type=F32)
-            total = term if total is None else total + term
-    return total
+def dot(lhs, rhs, dims):
+    return lax.dot_general(lhs, rhs, (dims, ((), ())), preferred_element_type=F32)
+
+
+def dot_rows(rows, table, dims):
+    stack = jnp.concatenate([part.astype(F32) for part in parts_of(rows)], axis=0).astype(BF16)
+    out = dot(stack, table, dims)
+    return out[0:8] + (out[8:16] + out[16:24])
 
 
 def slot_of(plane):
@@ -89,6 +90,7 @@
     own_zlo = src % 8
     goal_z = jnp.where(own_zlo % 2 == 0, own_zlo + 4, lax.rem(own_zlo + 11, 16))
     swap_z = jnp.where(own_zlo < 4, lax.rem(my_z + 12, 16), lax.rem(my_z + 4, 16))
+    my_spot = slab % 8
     native = core == upper
 
     def device(y, z, x, c):
@@ -97,11 +99,15 @@
     def is_me(dev):
         return (dev[0] == src) & (dev[1] == slab)
 
-    source_to = [device(my_y, goal_z + g % 2, g // 2, upper) for g in range(8)]
+    source_groups = [lax.rem(my_spot + k, 8) for k in range(8)]
     source_from = [(my_y * 8 + solved, core * 8 + i) for i in range(8)]
     near = [device(my_y, my_z, lax.rem(slab % 8 + j, 8) // 2, lax.rem(slab % 8 + j, 8) % 2) for j in range(1, 8)]
-    twin = [device(my_y, pair_z + 1 - parity, i // 2, i % 2) for i in range(8)]
-    native_to = [device(my_y, my_z, x, upper) for x in range(4)]
+    twin = []
+    for i in range(8):
+        spot = lax.rem(my_spot + i, 8)
+        twin.append(device(my_y, pair_z + 1 - parity, spot // 2, spot % 2))
+    native_x = [lax.rem(my_x + k, 4) for k in range(4)]
+    native_to = [device(my_y, my_z, x, upper) for x in native_x]
     beyond_to = device(my_y, swap_z, lax.rem(my_x + 4 - my_y, 4), upper)
     beyond_from = [device(my_y, swap_z, lax.rem(my_x + my_y, 4), c) for c in range(2)]
     y_peers = [(lax.rem(my_y + j, 4) * 8 + own_zlo, slab) for j in range(1, 4)]
@@ -110,12 +116,14 @@
     def plane_of(slot, half):
         return jnp.where(half == 0, slot, SLABS - 1 - slot)
 
+    row_slots = [lax.rem(2 * my_y + k, 8) for k in range(OWN_PLANES)]
     row_to = []
-    for q in range(OWN_PLANES):
+    for q in row_slots:
         p = plane_of(q, core) % 8
         row_to.append(device(my_x, my_z, p // 2, p % 2))
     row_from = [device(lax.rem(my_y + j, 4), my_z, my_y, c) for j in range(1, 4) for c in range(2)]
-    final_to = [[device(my_y, 8 * c + 4 * parity + h, my_x, core) for h in range(4)] for c in range(2)]
+    final_h = [lax.rem(my_z // 2 + k, 4) for k in range(4)]
+    final_to = [[device(my_y, 8 * c + 4 * parity + h, my_x, core) for h in final_h] for c in range(2)]
     final_from = [device(my_y, 2 * m + own_zlo // 4, my_x, core) for m in range(8)]
 
     barrier = pltpu.get_barrier_semaphore()
@@ -127,13 +135,16 @@
         def _():
             pl.semaphore_signal(barrier, inc=1, device_id=dev, device_id_type=MESH)
 
-    for dev in source_from + twin + row_from + near:
+    for dev in source_from:
         pl.semaphore_signal(barrier, inc=1, device_id=dev, device_id_type=MESH)
 
     @pl.when(jnp.logical_not(native))
     def _():
         for dev in beyond_from + y_peers:
             pl.semaphore_signal(barrier, inc=1, device_id=dev, device_id_type=MESH)
+
+    for dev in row_from + twin + near:
+        pl.semaphore_signal(barrier, inc=1, device_id=dev, device_id_type=MESH)
 
     loads = [
         pltpu.make_async_copy(ref, dst, i_sem.at[n])
@@ -172,7 +183,7 @@
         return pltpu.roll(jnp.where(lane < 127, here, ref[pl.ds(base - 1, SLOT), :]), 1, 1)
 
     def at(p):
-        return pl.multiple_of(p * SLOT, 8)
+        return p * SLOT if isinstance(p, int) else pl.multiple_of(p * SLOT, 8)
 
     for load in loads:
         load.wait()
@@ -204,6 +215,9 @@
     def arrived(ref, sem):
         pltpu.make_async_copy(ref, ref, sem).wait()
 
+    def source_slot(slot):
+        return source.at[pl.ds(at(slot + 1), SLOT), :]
+
     two = pl.ds(0, 2)
     my_slot = slot_of(slab)
     rows_leave = jnp.where(my_x == my_y, 0, 8)
@@ -212,20 +226,23 @@
         send.at[2 * lax.rem(my_x + 4 - my_y, 4) + parity, two], coef_recv.at[:, my_slot],
         o_send.at[0], o_recv.at[core], beyond_to,
     )]
-    for g, dev in enumerate(source_to):
-        sent.append(remote(send.at[g, 2], source.at[my_slot], s_send.at[g], s_recv.at[my_slot], dev))
-
-    def native_copy(x):
+    def native_copy(k):
         return remote_copy(
-            send.at[2 * x + parity, two], coef_recv.at[:, my_slot], k_send.at[x], k_recv.at[my_slot], native_to[x]
-        )
-
-    for x in range(4):
-
-        @pl.when(jnp.logical_not(is_me(native_to[x])))
+            send.at[2 * native_x[k] + parity, two], coef_recv.at[:, my_slot],
+            k_send.at[k], k_recv.at[my_slot], native_to[k],
+        )
+
+    for k in range(4):
+
+        @pl.when(jnp.logical_not(is_me(native_to[k])))
         def _():
-            native_copy(x).start()
-
+            native_copy(k).start()
+
+    for k, g in enumerate(source_groups):
+        sent.append(remote(
+            send.at[g, 2], source_slot(my_slot), s_send.at[k], s_recv.at[my_slot],
+            device(my_y, goal_z + g % 2, g // 2, upper),
+        ))
     sent.append(remote(
         pair_send, pair_recv, p_send.at[0], p_recv.at[0],
         device(my_y, goal_z + slab % 2, (slab % 8) // 2, upper),
@@ -235,6 +252,7 @@
     last = (PLANES + 1) * SLOT
     for start in (0, last):
         kappa[pl.ds(start, SLOT), :] = guard
+        source[pl.ds(start, SLOT), :] = guard
         for c in range(2):
             direc_a[c, pl.ds(start, SLOT), :] = guard
             direc_b[c, pl.ds(start, SLOT), :] = guard
@@ -263,38 +281,52 @@
 
     lane_hot[...] = (lax.broadcasted_iota(jnp.int32, (LANES, NDET), 0) == det_lane).astype(F32)
 
-    def pass_on(slot, both):
-        n = slot - 2
-        if both:
-            return remote_copy(
-                coef_recv.at[:, slot], coef_recv.at[:, SLABS - 1 - slot], t_send.at[n], t_recv.at[n], other_core
-            )
+    def coef_pass(slot):
         return remote_copy(
-            source.at[slot], source.at[SLABS - 1 - slot], u_send.at[n], u_recv.at[n], other_core
-        )
+            coef_recv.at[:, slot], coef_recv.at[:, SLABS - 1 - slot],
+            t_send.at[slot - 2], t_recv.at[slot - 2], other_core,
+        )
+
+    def coef_came(slot):
+        @pl.when(slot >= 2)
+        def _():
+            coef_pass(slot).start()
 
     @pl.when(native)
     def _():
         coef_recv[:, my_slot] = send[group, 0:2]
+        coef_came(my_slot)
         for j in range(1, 8):
             slot = lax.rem(my_slot + j, 8)
             arrived(coef_recv.at[:, slot], k_recv.at[slot])
+            coef_came(slot)
 
     @pl.when(jnp.logical_not(native))
     def _():
-        far_x = lax.rem(my_x + my_y, 4)
-        low = jnp.where(core == 0, 2 * far_x, 6 - 2 * far_x)
+        def first_slot(x):
+            return jnp.where(core == 0, 2 * x, 6 - 2 * x)
+
         for c in range(2):
-            slot = jnp.where(core == 0, 2 * far_x + c, 7 - 2 * far_x - c)
+            slot = jnp.where(core == 0, 2 * lax.rem(my_x + my_y, 4) + c, 7 - 2 * lax.rem(my_x + my_y, 4) - c)
             arrived(coef_recv.at[:, slot], o_recv.at[c])
-        strips = coef_recv.at[:, pl.ds(low, 2)]
+        slots = [pl.ds(first_slot(lax.rem(my_x + my_y + 4 - j, 4)), 2) for j in range(4)]
+        strips = coef_recv.at[:, slots[0]]
         across = [remote(strips, strips, g_send.at[j], g_recv.at[j], dev) for j, dev in enumerate(y_peers)]
+        for j in range(4):
+            if j:
+                arrived(coef_recv.at[:, slots[j]], g_recv.at[j - 1])
+            low = first_slot(lax.rem(my_x + my_y + 4 - j, 4))
+            for n in range(2):
+                coef_came(low + n)
         for copy in across:
-            copy.wait()
-
-    for slot in range(2, 8):
-        sent.append(pass_on(slot, True))
-        sent[-1].start()
+            copy.wait_send()
+
+    for slot in range(8):
+        arrived(source_slot(slot), s_recv.at[slot])
+        if slot >= 2:
+            sent.append(remote(
+                source_slot(slot), source_slot(SLABS - 1 - slot), u_send.at[slot - 2], u_recv.at[slot - 2], other_core
+            ))
     for n in range(6):
         arrived(coef_recv.at[:, OWN_PLANES + 5 - n], t_recv.at[n])
 
@@ -321,58 +353,69 @@
             coef[which, pl.ds(here, SLOT), :] = face * inside
         coef[6, pl.ds(here, SLOT), :] = diagonal
 
-    for slot in range(8):
-        arrived(source.at[slot], s_recv.at[slot])
-        if slot >= 2:
-            sent.append(pass_on(slot, False))
-            sent[-1].start()
     for n in range(6):
-        arrived(source.at[OWN_PLANES + 5 - n], u_recv.at[n])
+        arrived(source_slot(OWN_PLANES + 5 - n), u_recv.at[n])
 
     first, keeps, pushes = chebyshev_terms()
 
-    @pl.loop(0, PLANES, unroll=7)
-    def _(p):
-        base, here = at(p + 1), at(p)
-        b = source[p]
-        nothing = jnp.zeros_like(b)
-        resid[0, pl.ds(here, SLOT), :] = b
-        resid[1, pl.ds(here, SLOT), :] = nothing
-        direc_a[0, pl.ds(base, SLOT), :] = b * first
-        direc_a[1, pl.ds(base, SLOT), :] = nothing
-        field[0, 0, pl.ds(base, SLOT), :] = b * first
-        field[0, 1, pl.ds(base, SLOT), :] = nothing
-
-    def solve(out):
+    def spread_of(ref, base, cs, here):
+        up, down = ref[pl.ds(base + 1, SLOT), :], ref[pl.ds(base - 1, SLOT), :]
+        up_far, down_far = ref[pl.ds(base + 2, SLOT), :], ref[pl.ds(base - 2, SLOT), :]
+        return (
+            cs[0] * pltpu.roll(jnp.where(lane >= 32, up, up_far), 96, 1)
+            + cs[1] * pltpu.roll(jnp.where(lane < 96, down, down_far), 32, 1)
+            + cs[2] * pltpu.roll(jnp.where(lane >= 1, here, up), 127, 1)
+            + cs[3] * pltpu.roll(jnp.where(lane < 127, here, down), 1, 1)
+            + cs[4] * ref[pl.ds(base + SLOT, SLOT), :]
+            + cs[5] * ref[pl.ds(base - SLOT, SLOT), :]
+        )
+
+    def solve(out, rights):
         for sweep in range(SWEEPS - 1):
             keep, push = keeps[sweep], pushes[sweep]
             now, later = (direc_a, direc_b) if sweep % 2 == 0 else (direc_b, direc_a)
             count = PLANES - 1 - sweep
 
+            def first_sweep(p, kept):
+                here, base = at(p), at(p + 1)
+                cs = [coef[which, pl.ds(here, SLOT), :] for which in range(7)]
+                bs = [ref[pl.ds(base, SLOT), :] for ref in rights]
+                for c in range(2):
+                    if len(bs) == 1:
+                        turned = 0.0 if c == 0 else bs[0]
+                    else:
+                        turned = -bs[1] if c == 0 else bs[0]
+                    if c < len(bs):
+                        off = spread_of(rights[c], base, cs, bs[c])
+                        applied = cs[6] * bs[c] - off + frequency_shift * turned
+                        left = bs[c] - first * applied
+                        new = (keep * first) * bs[c] + push * left
+                        start = first * bs[c]
+                    else:
+                        left = (-first * frequency_shift) * turned
+                        new = push * left
+                        start = 0.0
+                    resid[c, pl.ds(here, SLOT), :] = left
+                    later[c, pl.ds(base, SLOT), :] = new
+                    if kept:
+                        field[out, c, pl.ds(base, SLOT), :] = start + new
+
             def one_plane(p, kept):
+                if sweep == 0:
+                    first_sweep(p, kept)
+                    return
                 here, base = at(p), at(p + 1)
                 cs = [coef[which, pl.ds(here, SLOT), :] for which in range(7)]
                 ds = [now[c, pl.ds(base, SLOT), :] for c in range(2)]
                 turned = (-ds[1], ds[0])
                 for c in range(2):
-
-                    def shifted(amount):
-                        return now[c, pl.ds(base + amount, SLOT), :]
-
-                    up, down = shifted(1), shifted(-1)
-                    off = (
-                        cs[0] * pltpu.roll(jnp.where(lane >= 32, up, shifted(2)), 96, 1)
-                        + cs[1] * pltpu.roll(jnp.where(lane < 96, down, shifted(-2)), 32, 1)
-                        + cs[2] * pltpu.roll(jnp.where(lane >= 1, ds[c], up), 127, 1)
-                        + cs[3] * pltpu.roll(jnp.where(lane < 127, ds[c], down), 1, 1)
-                        + cs[4] * shifted(SLOT)
-                        + cs[5] * shifted(-SLOT)
-                    )
+                    off = spread_of(now.at[c], base, cs, ds[c])
                     applied = cs[6] * ds[c] - off + frequency_shift * turned[c]
                     left = resid[c, pl.ds(here, SLOT), :] - applied
-                    resid[c, pl.ds(here, SLOT), :] = left
                     new = keep * ds[c] + push * left
-                    later[c, pl.ds(base, SLOT), :] = new
+                    if sweep < SWEEPS - 2:
+                        resid[c, pl.ds(here, SLOT), :] = left
+                        later[c, pl.ds(base, SLOT), :] = new
                     if kept:
                         field[out, c, pl.ds(base, SLOT), :] = field[out, c, pl.ds(base, SLOT), :] + new
 
@@ -386,15 +429,18 @@
                 def _(p):
                     one_plane(p, False)
 
-    solve(0)
+    solve(0, [source])
 
     whole = pl.ds(SLOT, FLAT)
     mine_rows = OWN_PLANES * SLOT
+    mine_planes = pl.ds(SLOT, mine_rows)
+    table = place[pl.ds(0, mine_rows), :]
+    both = jnp.concatenate([field[0, 0, mine_planes, :], field[0, 1, mine_planes, :]], axis=1)
+    high, middle, low = [dot(part, table, ((0,), (0,))) for part in parts_of(both)]
+    found = high + (middle + low)
     for c in range(2):
-        spread = dot_parts(
-            parts_of(field[0, c, pl.ds(SLOT, mine_rows), :]), (place[pl.ds(0, mine_rows), :],), ((0,), (0,))
-        )
-        reads[member, pl.ds(c, 1), :] = jnp.sum(spread * lane_hot[...], axis=0, keepdims=True) * owned
+        spread = found[LANES * c : LANES * (c + 1)] * lane_hot[...]
+        reads[member, pl.ds(c, 1), :] = jnp.sum(spread, axis=0, keepdims=True) * owned
     mine = reads.at[member]
     for i, dev in enumerate(twin + near):
         sent.append(remote(mine, mine, r_send.at[i], r_recv.at[member], dev))
@@ -407,7 +453,7 @@
         arrived(reads.at[other], r_recv.at[other])
     readings = jnp.sum(reads[...], axis=0)
     wide = jnp.concatenate([readings, jnp.zeros((6, NDET), F32)], axis=0)
-    model = dot_parts(parts_of(wide), (pair_hot[...],), ((1,), (0,)))
+    model = dot_rows(wide, pair_hot[...], ((1,), (0,)))
     active = pair_recv[3:4]
     conj = jnp.concatenate(
         [
@@ -417,24 +463,26 @@
         ],
         axis=0,
     )
-    weights = dot_parts(parts_of(conj), (pair_hot[...],), ((1,), (1,)))
+    weights = dot_rows(conj, pair_hot[...], ((1,), (1,)))
+    hot = lane_hot[...]
+    right = None
+    for part in parts_of(weights):
+        part = part.astype(F32)
+        piece = jnp.concatenate([hot * part[0:1], hot * part[1:2]], axis=0).astype(BF16)
+        term = dot(place[...], piece, ((1,), (1,)))
+        right = term if right is None else right + term
     for c in range(2):
-        hot = lane_hot[...]
-        pieces = [(hot * part.astype(F32)).astype(BF16) for part in parts_of(weights[c : c + 1])]
-        right = dot_parts((place[...],), pieces, ((1,), (1,)))
-        resid[c] = right
-        direc_a[c, whole, :] = right * first
-        field[1, c, whole, :] = right * first
-
-    solve(1)
-
-    def row_copy(q):
+        direc_a[c, whole, :] = right[:, LANES * c : LANES * (c + 1)]
+
+    solve(1, [direc_a.at[0], direc_a.at[1]])
+
+    def row_copy(k):
         return remote_copy(
-            ysend.at[q], yrecv.at[core, my_y], y_send.at[q], y_recv.at[core, my_y], row_to[q]
-        )
-
-    for q in range(OWN_PLANES):
-        base = (q + 1) * SLOT
+            ysend.at[k], yrecv.at[core, my_y], y_send.at[k], y_recv.at[core, my_y], row_to[k]
+        )
+
+    for k, q in enumerate(row_slots):
+        base = at(q + 1)
         refs = [[field.at[a, c] for c in range(2)] for a in range(2)]
         here = [[refs[a][c][pl.ds(base, SLOT), :] for c in range(2)] for a in range(2)]
         sides = (
@@ -449,26 +497,26 @@
         for side in sides:
             gap = [[here[a][c] - side(refs[a][c], base) for c in range(2)] for a in range(2)]
             total = total + gap[0][0] * gap[1][0] - gap[0][1] * gap[1][1]
-        grads[q, 0] = here[0][0] * here[1][0] - here[0][1] * here[1][1]
-        grads[q, 1] = total
+        grads[k, 0] = here[0][0] * here[1][0] - here[0][1] * here[1][1]
+        grads[k, 1] = total
         for out in range(2):
-            low, high = grads[q, out, pl.ds(7, 32), :], grads[q, out, pl.ds(8, 32), :]
+            low, high = grads[k, out, pl.ds(7, 32), :], grads[k, out, pl.ds(8, 32), :]
             rows = pltpu.roll(jnp.where(lane[0:32] >= 64, low, high), 64, 1)
-            ysend[q, pl.ds(25 * out, 25), :] = rows[0:25]
-        ysend[q, pl.ds(50, 6), :] = jnp.zeros((6, LANES), F32)
-        stays = is_me(row_to[q])
+            ysend[k, pl.ds(25 * out, 25), :] = rows[0:25]
+        ysend[k, pl.ds(50, 6), :] = jnp.zeros((6, LANES), F32)
+        stays = is_me(row_to[k])
 
         @pl.when(jnp.logical_not(stays))
         def _():
-            row_copy(q).start()
+            row_copy(k).start()
 
         @pl.when(stays)
         def _():
-            pltpu.make_async_copy(ysend.at[q], yrecv.at[core, my_y], y_recv.at[core, my_y]).start()
-
-    def final_copy(c, h):
+            pltpu.make_async_copy(ysend.at[k], yrecv.at[core, my_y], y_recv.at[core, my_y]).start()
+
+    def final_copy(c, k):
         return remote_copy(
-            fsend.at[c, h], frecv.at[my_z // 2], f_send.at[4 * c + h], f_recv.at[my_z // 2], final_to[c][h]
+            fsend.at[c, final_h[k]], frecv.at[my_z // 2], f_send.at[4 * c + k], f_recv.at[my_z // 2], final_to[c][k]
         )
 
     for c in range(2):
@@ -483,28 +531,31 @@
                     fsend[c, h, out] = low
                 else:
                     fsend[c, h, out] = pltpu.roll(jnp.where(lane[0:8] >= 32 * h, low, high), 128 - 32 * h, 1)
-            own = is_me(final_to[c][h])
+        for k in range(4):
+            own = is_me(final_to[c][k])
 
             @pl.when(jnp.logical_not(own))
             def _():
-                final_copy(c, h).start()
+                final_copy(c, k).start()
 
             @pl.when(own)
             def _():
-                pltpu.make_async_copy(fsend.at[c, h], frecv.at[my_z // 2], f_recv.at[my_z // 2]).start()
-
-    for x in range(4):
-
-        @pl.when(jnp.logical_not(is_me(native_to[x])))
+                pltpu.make_async_copy(fsend.at[c, final_h[k]], frecv.at[my_z // 2], f_recv.at[my_z // 2]).start()
+
+    for k in range(4):
+
+        @pl.when(jnp.logical_not(is_me(native_to[k])))
         def _():
-            native_copy(x).wait_send()
-
-    for q in range(OWN_PLANES):
-
-        @pl.when(jnp.logical_not(is_me(row_to[q])))
+            native_copy(k).wait_send()
+
+    for k in range(OWN_PLANES):
+
+        @pl.when(jnp.logical_not(is_me(row_to[k])))
         def _():
-            row_copy(q).wait_send()
-
+            row_copy(k).wait_send()
+
+    for slot in range(2, 8):
+        coef_pass(slot).wait_send()
     for copy in sent:
         copy.wait_send()
     for m in range(8):
@@ -517,11 +568,11 @@
             out_ref[out, 0:1, pl.ds(128 * k, 128)] = total[k : k + 1]
         out_ref[out, 0:1, pl.ds(768, 32)] = total[6:7, 0:32]
     for c in range(2):
-        for h in range(4):
-
-            @pl.when(jnp.logical_not(is_me(final_to[c][h])))
+        for k in range(4):
+
+            @pl.when(jnp.logical_not(is_me(final_to[c][k])))
             def _():
-                final_copy(c, h).wait_send()
+                final_copy(c, k).wait_send()
 
 
 def body(source_field, kappa, absorb, det_cell, pair_det, pair_count, measured):
@@ -543,7 +594,7 @@
             pltpu.VMEM((3, TALL, LANES), F32),
             pltpu.VMEM((8, 3, SLOT, LANES), F32),
             pltpu.VMEM((2, PLANES, SLOT, LANES), F32),
-            pltpu.VMEM((PLANES, SLOT, LANES), F32),
+            pltpu.VMEM((STACKED, LANES), F32),
             pltpu.VMEM((STACKED, LANES), F32),
             pltpu.VMEM((7, FLAT, LANES), F32),
             pltpu.VMEM((2, STACKED, LANES), F32),

time: 63.4 us -> 62 us (0.978)
  the two profiles are of different devices: /device:TPU:25 before, /device:TPU:1 now
where the time goes in v5:
time: 62 us; the launch traced here: 61.2 us
  Pallas kernels  58.6 us (95%)
  between operations  1.29 us (2%)
  other arithmetic  1.27 us (2%)
    pallas_call x1, Pallas kernels, body(): pl.pallas_call(kernel, out_shape=out, in_specs=[hbm] * 7, out_specs=vmem,...  58.6 us
    mul x1, other arithmetic, body(): return (-sums[0], -0.5 * sums[1])  1.27 us

profile of v5, /device:TPU:1, one launch (start us, length us, event | category | flops | bytes accessed | tf_op | source)
XLA Modules:
  0.0 61.2 jit_solution(5903089633847404612)
XLA Ops:
  1.3 58.6 %shard_map.86 = f32[2,1,800]{2,1,0:T(1,128)} custom-call(s32[1]{0:T(128)S(6)} %copy.9.count_hbm, f32[200,128]{1,0:T(8,128)} %bitcast.8, f32[200,128]{1,0:T(8,128)} %bitcast.9, f32[200,128]{1,0:T(8,128)} %bitcast.10, s32[1,512]{1,0:T(1,128)} %bitcast.11, s32[1,256]{1,0:T(1,128)} %pair_hbm.1, f32[2,1,256]{2,1,0:T(1,128)} %measured_hbm.1), custom_call_target="tpu_custom_call" | custom-call | tf_op jit(solution)/shard_map/pallas_call | solution.py:583
  59.9 1.3 %multiply_bitcast_fusion = (f32[1,800]{1,0:T(1,128)}, f32[1,800]{1,0:T(1,128)}) fusion(f32[2,1,800]{2,1,0:T(1,128)} %shard_map.86), kind=kLoop, calls=%fused_computation | loop fusion | flops 1600 | bytes 12800 | tf_op jit(solution)/shard_map/mul | solution.py:633

commit v6 on v5

--- a/solution.py
+++ b/solution.py
@@ -82,15 +82,18 @@
     my_x = (slab % 8) // 2
     core = slab % 2
     upper = my_z // 8
-    parity = my_z % 2
-    pair_z = my_z - parity
+    odd = my_z % 2
+    pair_z = my_z - odd
+    parity = jnp.where(upper == 0, odd, 1 - odd)
     group = my_x * 2 + parity
     member = group * 2 + core
     solved = jnp.where((pair_z >= 4) & (pair_z <= 10), pair_z - 4, lax.rem(pair_z + 5, 16))
     own_zlo = src % 8
     goal_z = jnp.where(own_zlo % 2 == 0, own_zlo + 4, lax.rem(own_zlo + 11, 16))
+    def goal_of(half):
+        return goal_z + jnp.where(goal_z < 8, half, 1 - half)
+
     swap_z = jnp.where(own_zlo < 4, lax.rem(my_z + 12, 16), lax.rem(my_z + 4, 16))
-    my_spot = slab % 8
     native = core == upper
 
     def device(y, z, x, c):
@@ -99,14 +102,13 @@
     def is_me(dev):
         return (dev[0] == src) & (dev[1] == slab)
 
-    source_groups = [lax.rem(my_spot + k, 8) for k in range(8)]
+    far_x = [lax.rem(my_x + step, 4) for step in (2, 1, 3, 0)]
+    far_spots = [(x, c) for x in far_x for c in range(2)]
+    source_groups = [2 * x + c for x, c in far_spots]
     source_from = [(my_y * 8 + solved, core * 8 + i) for i in range(8)]
-    near = [device(my_y, my_z, lax.rem(slab % 8 + j, 8) // 2, lax.rem(slab % 8 + j, 8) % 2) for j in range(1, 8)]
-    twin = []
-    for i in range(8):
-        spot = lax.rem(my_spot + i, 8)
-        twin.append(device(my_y, pair_z + 1 - parity, spot // 2, spot % 2))
-    native_x = [lax.rem(my_x + k, 4) for k in range(4)]
+    near = [device(my_y, my_z, x, c) for x, c in far_spots[:6]] + [device(my_y, my_z, my_x, 1 - core)]
+    twin = [device(my_y, pair_z + 1 - odd, x, c) for x, c in far_spots]
+    native_x = far_x
     native_to = [device(my_y, my_z, x, upper) for x in native_x]
     beyond_to = device(my_y, swap_z, lax.rem(my_x + 4 - my_y, 4), upper)
     beyond_from = [device(my_y, swap_z, lax.rem(my_x + my_y, 4), c) for c in range(2)]
@@ -116,15 +118,18 @@
     def plane_of(slot, half):
         return jnp.where(half == 0, slot, SLABS - 1 - slot)
 
-    row_slots = [lax.rem(2 * my_y + k, 8) for k in range(OWN_PLANES)]
+    row_slots = [jnp.where(core == 0, 2 * x + c, 7 - 2 * x - c) for x, c in far_spots]
     row_to = []
     for q in row_slots:
         p = plane_of(q, core) % 8
         row_to.append(device(my_x, my_z, p // 2, p % 2))
     row_from = [device(lax.rem(my_y + j, 4), my_z, my_y, c) for j in range(1, 4) for c in range(2)]
-    final_h = [lax.rem(my_z // 2 + k, 4) for k in range(4)]
+    final_h = list(range(4))
     final_to = [[device(my_y, 8 * c + 4 * parity + h, my_x, core) for h in final_h] for c in range(2)]
-    final_from = [device(my_y, 2 * m + own_zlo // 4, my_x, core) for m in range(8)]
+    final_half = own_zlo // 4
+    final_from = [
+        device(my_y, 2 * m + (final_half if m < 4 else 1 - final_half), my_x, core) for m in range(8)
+    ]
 
     barrier = pltpu.get_barrier_semaphore()
     to_self = jnp.int32(0)
@@ -223,7 +228,7 @@
     rows_leave = jnp.where(my_x == my_y, 0, 8)
     pl.semaphore_wait(barrier, 8 + 8 + 7 + 1 + 8 - to_self + rows_leave + jnp.where(native, 0, 3))
     sent = [remote(
-        send.at[2 * lax.rem(my_x + 4 - my_y, 4) + parity, two], coef_recv.at[:, my_slot],
+        send.at[2 * lax.rem(my_x + 4 - my_y, 4) + 1 - parity, two], coef_recv.at[:, my_slot],
         o_send.at[0], o_recv.at[core], beyond_to,
     )]
     def native_copy(k):
@@ -241,11 +246,11 @@
     for k, g in enumerate(source_groups):
         sent.append(remote(
             send.at[g, 2], source_slot(my_slot), s_send.at[k], s_recv.at[my_slot],
-            device(my_y, goal_z + g % 2, g // 2, upper),
+            device(my_y, goal_of(g % 2), g // 2, upper),
         ))
     sent.append(remote(
         pair_send, pair_recv, p_send.at[0], p_recv.at[0],
-        device(my_y, goal_z + slab % 2, (slab % 8) // 2, upper),
+        device(my_y, goal_of(slab % 2), (slab % 8) // 2, upper),
     ))
 
     guard = jnp.zeros((SLOT, LANES), F32)

time: 62 us -> 61.4 us (level); the launches traced: 61.2 us -> 61.3 us
  no operation moved by 1% of the time
where the time goes in v6:
time: 61.4 us; the launch traced here: 61.3 us
  Pallas kernels  58.7 us (96%)
  between operations  1.29 us (2%)
  other arithmetic  1.27 us (2%)
    pallas_call x1, Pallas kernels, body(): pl.pallas_call(kernel, out_shape=out, in_specs=[hbm] * 7, out_specs=vmem,...  58.7 us
    mul x1, other arithmetic, body(): return (-sums[0], -0.5 * sums[1])  1.27 us

profile of v6, /device:TPU:1, one launch (start us, length us, event | category | flops | bytes accessed | tf_op | source)
XLA Modules:
  0.0 61.3 jit_solution(12985279527358121580)
XLA Ops:
  1.3 58.7 %shard_map.86 = f32[2,1,800]{2,1,0:T(1,128)} custom-call(s32[1]{0:T(128)S(6)} %copy.9.count_hbm, f32[200,128]{1,0:T(8,128)} %bitcast.8, f32[200,128]{1,0:T(8,128)} %bitcast.9, f32[200,128]{1,0:T(8,128)} %bitcast.10, s32[1,512]{1,0:T(1,128)} %bitcast.11, s32[1,256]{1,0:T(1,128)} %pair_hbm.1, f32[2,1,256]{2,1,0:T(1,128)} %measured_hbm.1), custom_call_target="tpu_custom_call" | custom-call | tf_op jit(solution)/shard_map/pallas_call | solution.py:588
  60.0 1.3 %multiply_bitcast_fusion = (f32[1,800]{1,0:T(1,128)}, f32[1,800]{1,0:T(1,128)}) fusion(f32[2,1,800]{2,1,0:T(1,128)} %shard_map.86), kind=kLoop, calls=%fused_computation | loop fusion | flops 1600 | bytes 12800 | tf_op jit(solution)/shard_map/mul | solution.py:638

commit v7 on v6

--- a/solution.py
+++ b/solution.py
@@ -11,6 +11,8 @@
 PAIRS = 256
 SLABS = 16
 HALO = 6
+INNER = 32
+INNER_AT = 4
 OWN_ROWS = 20
 OWN_PLANES = 8
 PLANES = OWN_PLANES + HALO
@@ -172,20 +174,24 @@
     xm_in = (row_in & (real_row > 0)).astype(F32)
     yp_in = (col < NY - 1).astype(F32)
     ym_in = (col > 0).astype(F32)
-
-    def x_plus(ref, base):
-        near_row, far_row = ref[pl.ds(base + 1, SLOT), :], ref[pl.ds(base + 2, SLOT), :]
-        return pltpu.roll(jnp.where(lane >= 32, near_row, far_row), 96, 1)
-
-    def x_minus(ref, base):
-        near_row, far_row = ref[pl.ds(base - 1, SLOT), :], ref[pl.ds(base - 2, SLOT), :]
-        return pltpu.roll(jnp.where(lane < 96, near_row, far_row), 32, 1)
-
-    def y_plus(ref, base, here):
-        return pltpu.roll(jnp.where(lane >= 1, here, ref[pl.ds(base + 1, SLOT), :]), 127, 1)
-
-    def y_minus(ref, base, here):
-        return pltpu.roll(jnp.where(lane < 127, here, ref[pl.ds(base - 1, SLOT), :]), 1, 1)
+    inner_flat = flat[0:INNER] + INNER_AT * LANES
+    inner_col = inner_flat - (((inner_flat >> 5) * 205) >> 10) * NY
+    yp_inner = (inner_col < NY - 1).astype(F32)
+    ym_inner = (inner_col > 0).astype(F32)
+
+    def x_plus(ref, base, size=SLOT):
+        near_row, far_row = ref[pl.ds(base + 1, size), :], ref[pl.ds(base + 2, size), :]
+        return pltpu.roll(jnp.where(lane[0:size] >= 32, near_row, far_row), 96, 1)
+
+    def x_minus(ref, base, size=SLOT):
+        near_row, far_row = ref[pl.ds(base - 1, size), :], ref[pl.ds(base - 2, size), :]
+        return pltpu.roll(jnp.where(lane[0:size] < 96, near_row, far_row), 32, 1)
+
+    def y_plus(ref, base, here, size=SLOT):
+        return pltpu.roll(jnp.where(lane[0:size] >= 1, here, ref[pl.ds(base + 1, size), :]), 127, 1)
+
+    def y_minus(ref, base, here, size=SLOT):
+        return pltpu.roll(jnp.where(lane[0:size] < 127, here, ref[pl.ds(base - 1, size), :]), 1, 1)
 
     def at(p):
         return p * SLOT if isinstance(p, int) else pl.multiple_of(p * SLOT, 8)
@@ -363,16 +369,14 @@
 
     first, keeps, pushes = chebyshev_terms()
 
-    def spread_of(ref, base, cs, here):
-        up, down = ref[pl.ds(base + 1, SLOT), :], ref[pl.ds(base - 1, SLOT), :]
-        up_far, down_far = ref[pl.ds(base + 2, SLOT), :], ref[pl.ds(base - 2, SLOT), :]
+    def spread_of(ref, base, cs, here, size=SLOT):
         return (
-            cs[0] * pltpu.roll(jnp.where(lane >= 32, up, up_far), 96, 1)
-            + cs[1] * pltpu.roll(jnp.where(lane < 96, down, down_far), 32, 1)
-            + cs[2] * pltpu.roll(jnp.where(lane >= 1, here, up), 127, 1)
-            + cs[3] * pltpu.roll(jnp.where(lane < 127, here, down), 1, 1)
-            + cs[4] * ref[pl.ds(base + SLOT, SLOT), :]
-            + cs[5] * ref[pl.ds(base - SLOT, SLOT), :]
+            cs[0] * x_plus(ref, base, size)
+            + cs[1] * x_minus(ref, base, size)
+            + cs[2] * y_plus(ref, base, here, size)
+            + cs[3] * y_minus(ref, base, here, size)
+            + cs[4] * ref[pl.ds(base + SLOT, size), :]
+            + cs[5] * ref[pl.ds(base - SLOT, size), :]
         )
 
     def solve(out, rights):
@@ -409,20 +413,21 @@
                 if sweep == 0:
                     first_sweep(p, kept)
                     return
-                here, base = at(p), at(p + 1)
-                cs = [coef[which, pl.ds(here, SLOT), :] for which in range(7)]
-                ds = [now[c, pl.ds(base, SLOT), :] for c in range(2)]
+                skip, size = (INNER_AT, INNER) if sweep >= SWEEPS - 3 else (0, SLOT)
+                here, base = at(p) + skip, at(p + 1) + skip
+                cs = [coef[which, pl.ds(here, size), :] for which in range(7)]
+                ds = [now[c, pl.ds(base, size), :] for c in range(2)]
                 turned = (-ds[1], ds[0])
                 for c in range(2):
-                    off = spread_of(now.at[c], base, cs, ds[c])
+                    off = spread_of(now.at[c], base, cs, ds[c], size)
                     applied = cs[6] * ds[c] - off + frequency_shift * turned[c]
-                    left = resid[c, pl.ds(here, SLOT), :] - applied
+                    left = resid[c, pl.ds(here, size), :] - applied
                     new = keep * ds[c] + push * left
                     if sweep < SWEEPS - 2:
-                        resid[c, pl.ds(here, SLOT), :] = left
-                        later[c, pl.ds(base, SLOT), :] = new
+                        resid[c, pl.ds(here, size), :] = left
+                        later[c, pl.ds(base, size), :] = new
                     if kept:
-                        field[out, c, pl.ds(base, SLOT), :] = field[out, c, pl.ds(base, SLOT), :] + new
+                        field[out, c, pl.ds(base, size), :] = field[out, c, pl.ds(base, size), :] + new
 
             @pl.loop(0, OWN_PLANES + 1, unroll=OWN_PLANES + 1)
             def _(p):
@@ -487,26 +492,26 @@
         )
 
     for k, q in enumerate(row_slots):
-        base = at(q + 1)
+        base = at(q + 1) + INNER_AT
         refs = [[field.at[a, c] for c in range(2)] for a in range(2)]
-        here = [[refs[a][c][pl.ds(base, SLOT), :] for c in range(2)] for a in range(2)]
+        here = [[refs[a][c][pl.ds(base, INNER), :] for c in range(2)] for a in range(2)]
         sides = (
-            x_plus,
-            x_minus,
-            lambda ref, b: y_plus(ref, b, ref[pl.ds(b, SLOT), :]) * yp_in,
-            lambda ref, b: y_minus(ref, b, ref[pl.ds(b, SLOT), :]) * ym_in,
-            lambda ref, b: ref[pl.ds(b + SLOT, SLOT), :],
-            lambda ref, b: ref[pl.ds(b - SLOT, SLOT), :],
-        )
-        total = jnp.zeros((SLOT, LANES), F32)
+            lambda ref, b: x_plus(ref, b, INNER),
+            lambda ref, b: x_minus(ref, b, INNER),
+            lambda ref, b: y_plus(ref, b, ref[pl.ds(b, INNER), :], INNER) * yp_inner,
+            lambda ref, b: y_minus(ref, b, ref[pl.ds(b, INNER), :], INNER) * ym_inner,
+            lambda ref, b: ref[pl.ds(b + SLOT, INNER), :],
+            lambda ref, b: ref[pl.ds(b - SLOT, INNER), :],
+        )
+        total = jnp.zeros((INNER, LANES), F32)
         for side in sides:
             gap = [[here[a][c] - side(refs[a][c], base) for c in range(2)] for a in range(2)]
             total = total + gap[0][0] * gap[1][0] - gap[0][1] * gap[1][1]
         grads[k, 0] = here[0][0] * here[1][0] - here[0][1] * here[1][1]
         grads[k, 1] = total
         for out in range(2):
-            low, high = grads[k, out, pl.ds(7, 32), :], grads[k, out, pl.ds(8, 32), :]
-            rows = pltpu.roll(jnp.where(lane[0:32] >= 64, low, high), 64, 1)
+            low, high = grads[k, out, pl.ds(3, 28), :], grads[k, out, pl.ds(4, 28), :]
+            rows = pltpu.roll(jnp.where(lane[0:28] >= 64, low, high), 64, 1)
             ysend[k, pl.ds(25 * out, 25), :] = rows[0:25]
         ysend[k, pl.ds(50, 6), :] = jnp.zeros((6, LANES), F32)
         stays = is_me(row_to[k])
@@ -606,7 +611,7 @@
             pltpu.VMEM((2, STACKED, LANES), F32),
             pltpu.VMEM((2, FLAT, LANES), F32),
             pltpu.VMEM((2, 2, STACKED, LANES), F32),
-            pltpu.VMEM((OWN_PLANES, 2, SLOT, LANES), F32),
+            pltpu.VMEM((OWN_PLANES, 2, INNER, LANES), F32),
             pltpu.VMEM((FLAT, NDET), BF16),
             pltpu.VMEM((LANES, NDET), F32),
             pltpu.VMEM((NDET, PAIRS), BF16),

time: 61.4 us -> 60.9 us (level)
  no operation moved by 1% of the time
where the time goes in v7:
time: 60.9 us; the launch traced here: 60.7 us
  Pallas kernels  58.2 us (96%)
  between operations  1.29 us (2%)
  other arithmetic  1.27 us (2%)
    pallas_call x1, Pallas kernels, body(): pl.pallas_call(kernel, out_shape=out, in_specs=[hbm] * 7, out_specs=vmem,...  58.2 us
    mul x1, other arithmetic, body(): return (-sums[0], -0.5 * sums[1])  1.27 us

profile of v7, /device:TPU:1, one launch (start us, length us, event | category | flops | bytes accessed | tf_op | source)
XLA Modules:
  0.0 60.7 jit_solution(4337044033001036280)
XLA Ops:
  1.3 58.2 %shard_map.86 = f32[2,1,800]{2,1,0:T(1,128)} custom-call(s32[1]{0:T(128)S(6)} %copy.9.count_hbm, f32[200,128]{1,0:T(8,128)} %bitcast.8, f32[200,128]{1,0:T(8,128)} %bitcast.9, f32[200,128]{1,0:T(8,128)} %bitcast.10, s32[1,512]{1,0:T(1,128)} %bitcast.11, s32[1,256]{1,0:T(1,128)} %pair_hbm.1, f32[2,1,256]{2,1,0:T(1,128)} %measured_hbm.1), custom_call_target="tpu_custom_call" | custom-call | tf_op jit(solution)/shard_map/pallas_call | solution.py:593
  59.5 1.3 %multiply_bitcast_fusion = (f32[1,800]{1,0:T(1,128)}, f32[1,800]{1,0:T(1,128)}) fusion(f32[2,1,800]{2,1,0:T(1,128)} %shard_map.86), kind=kLoop, calls=%fused_computation | loop fusion | flops 1600 | bytes 12800 | tf_op jit(solution)/shard_map/mul | solution.py:643

commit v8 on v7

--- a/solution.py
+++ b/solution.py
@@ -476,7 +476,7 @@
     weights = dot_rows(conj, pair_hot[...], ((1,), (1,)))
     hot = lane_hot[...]
     right = None
-    for part in parts_of(weights):
+    for part in parts_of(weights)[:2]:
         part = part.astype(F32)
         piece = jnp.concatenate([hot * part[0:1], hot * part[1:2]], axis=0).astype(BF16)
         term = dot(place[...], piece, ((1,), (1,)))

time: 60.9 us -> 60.8 us (level)
  no operation moved by 1% of the time
where the time goes in v8:
time: 60.8 us; the launch traced here: 60.6 us
  Pallas kernels  58 us (95%)
  between operations  1.29 us (2%)
  other arithmetic  1.27 us (2%)
    pallas_call x1, Pallas kernels, body(): pl.pallas_call(kernel, out_shape=out, in_specs=[hbm] * 7, out_specs=vmem,...  58 us
    mul x1, other arithmetic, body(): return (-sums[0], -0.5 * sums[1])  1.27 us

profile of v8, /device:TPU:1, one launch (start us, length us, event | category | flops | bytes accessed | tf_op | source)
XLA Modules:
  0.0 60.6 jit_solution(6740462617185901555)
XLA Ops:
  1.3 58.0 %shard_map.86 = f32[2,1,800]{2,1,0:T(1,128)} custom-call(s32[1]{0:T(128)S(6)} %copy.9.count_hbm, f32[200,128]{1,0:T(8,128)} %bitcast.8, f32[200,128]{1,0:T(8,128)} %bitcast.9, f32[200,128]{1,0:T(8,128)} %bitcast.10, s32[1,512]{1,0:T(1,128)} %bitcast.11, s32[1,256]{1,0:T(1,128)} %pair_hbm.1, f32[2,1,256]{2,1,0:T(1,128)} %measured_hbm.1), custom_call_target="tpu_custom_call" | custom-call | tf_op jit(solution)/shard_map/pallas_call | solution.py:593
  59.3 1.3 %multiply_bitcast_fusion = (f32[1,800]{1,0:T(1,128)}, f32[1,800]{1,0:T(1,128)}) fusion(f32[2,1,800]{2,1,0:T(1,128)} %shard_map.86), kind=kLoop, calls=%fused_computation | loop fusion | flops 1600 | bytes 12800 | tf_op jit(solution)/shard_map/mul | solution.py:643
